TPU v7x, 128 devices: a whole 4x4x4 slice. The times are simulated.
128 devices in a mesh: phase: 4 (over x_hi, core), tile: 32 (over x_lo, z, y).
Axes of the slice: x: 4 (x_hi: 2, x_lo: 2; x = x_hi * 2 + x_lo), y: 4, z: 4, core: 2. Of those that a mesh axis runs over, the one named last changes fastest.
Arguments:
- adjoint_in: float32 [16, 4, 256, 128, 128], P('phase', None, 'tile'), may hold values from -6 to 6
- velocity: bfloat16 [16, 3, 256, 128, 128], P('phase', None, 'tile'), may hold values from -4 to 4
- temp_grad: bfloat16 [16, 3, 256, 128, 128], P('phase', None, 'tile'), may hold values from -3 to 3
- heat_weight: bfloat16 [16, 256, 128, 128], P('phase', 'tile'), may hold values from -6 to 6
- density: float32 [256, 128, 128], P('tile'), may hold values from 0.02 to 1
- cell_kind: int32 [256, 128, 128], P('tile'), may hold values from 0 to 2
- inlet: int32 [256, 128, 128], P('tile'), may hold values 0 or 1
Outputs:
- adjoint_out: float32 [16, 4, 256, 128, 128], P('phase', None, 'tile')
- sensitivity: float32 [256, 128, 128], P('tile')
All inputs are finite; a program needn't handle non-finite values. No bound on the sum of `inlet` on one device may be relied on, other than what follows from the above.
Results may differ from a plain program's by a relative error of at most 0.0003.
Values may be sent and summed in bfloat16 or wider, within the bound.
A program may use at most 320 MiB of HBM per device.

v0:
```python
import jax
import jax.numpy as jnp
from jax import lax
from jax.sharding import PartitionSpec as P

STEPS = 3


def passed_along(block, axis, distance):
    devices = range(lax.axis_size(axis))
    route = [((i - distance) % len(devices), i) for i in devices]
    return lax.ppermute(block, axis, route)


def padded_2(shard, sides, width):
    for axis, dim in sides:
        peers, length = (lax.axis_size(axis), shard.shape[dim])
        up = [(i, (i + 1) % peers) for i in range(peers - 1)]
        down = [(j, i) for i, j in up]
        last = lax.slice_in_dim(shard, length - width, length, axis=dim)
        first = lax.slice_in_dim(shard, 0, width, axis=dim)
        before = lax.ppermute(last, axis, up)
        after = lax.ppermute(first, axis, down)
        shard = jnp.concatenate([before, shard, after], axis=dim)
    return shard


def coefficients(density, cell_kind):
    rho = jnp.where(
        cell_kind == 0,
        density,
        jnp.where(cell_kind == 2, jnp.ones_like(density), jnp.zeros_like(density)),
    )
    penalty = 0.5 * 0.5 * (1.0 - rho) / (0.5 + rho)
    slope = jnp.where(
        cell_kind == 0, -0.5 * 0.5 * 1.5 / ((0.5 + rho) * (0.5 + rho)), jnp.zeros_like(rho)
    )
    return (penalty, slope)


def advance(extended, flow, temp_grad, heat, penalty, keep):
    center = extended[..., 1:-1, :, :]
    lower = extended[..., :-2, :, :]
    upper = extended[..., 2:, :, :]
    widths = [(0, 0)] * (center.ndim - 2) + [(1, 1), (1, 1)]
    padded = jnp.pad(center, widths)
    left = padded[..., :-2, 1:-1]
    right = padded[..., 2:, 1:-1]
    below = padded[..., 1:-1, :-2]
    above = padded[..., 1:-1, 2:]
    laplace = upper + lower + left + right + below + above - 6.0 * center
    momentum = center[..., 0:3, :, :, :]
    thermal = center[..., 3, :, :, :]
    grad_x = 0.5 * (right - left)[..., 3, :, :, :]
    grad_y = 0.5 * (upper - lower)[..., 3, :, :, :]
    grad_z = 0.5 * (above - below)[..., 3, :, :, :]
    speed = flow.astype(jnp.float32)
    advect = (
        speed[..., 0, :, :, :] * grad_x
        + speed[..., 1, :, :, :] * grad_y
        + speed[..., 2, :, :, :] * grad_z
    )
    coupling = jnp.expand_dims(thermal, -4) * temp_grad.astype(jnp.float32)
    mom_new = keep * (momentum + 0.12 * laplace[..., 0:3, :, :, :] - penalty * momentum - coupling)
    heat_new = thermal + 0.12 * laplace[..., 3, :, :, :] + 0.2 * advect + heat.astype(jnp.float32)
    return jnp.concatenate([mom_new, jnp.expand_dims(heat_new, -4)], axis=-4)


def on_device(adjoint_in, velocity, temp_grad, heat_weight, density, cell_kind, inlet):
    penalty, slope = coefficients(density, cell_kind)
    keep = (1 - inlet).astype(jnp.float32)
    state = adjoint_in
    for step in range(STEPS):
        first = passed_along(state[0:1], "phase", -1)
        later = jnp.concatenate([state[1:], first], axis=0)
        extended = padded_2(later, (("tile", 2),), 1)
        state = advance(extended, velocity, temp_grad, heat_weight, penalty, keep)
    terms = jnp.sum(velocity.astype(jnp.float32) * state[:, 0:3], axis=(0, 1))
    summed = lax.psum(terms, "phase")
    return (state, slope * summed)


def solution(mesh):
    return jax.shard_map(
        on_device,
        mesh=mesh,
        in_specs=(
            P("phase", None, "tile", None, None),
            P("phase", None, "tile", None, None),
            P("phase", None, "tile", None, None),
            P("phase", "tile", None, None),
            P("tile", None, None),
            P("tile", None, None),
            P("tile", None, None),
        ),
        out_specs=(P("phase", None, "tile", None, None), P("tile", None, None)),
        check_vma=False,
    )
```

profile of v0, /device:TPU:3, one launch (start us, length us, event | category | flops | bytes accessed | tf_op | source)
XLA Modules:
  0.0 388.1 jit_solution(7303062004474575305)
XLA Ops:
  9.7 3.5 copy_dynamic-update-slice_fusion
  13.3 22.7 %collective-permute-done = f32[1,4,8,128,128]{4,3,2,0,1:T(8,128)S(1)} collective-permute-done((f32[1,4,8,128,128]{4,3,2,0,1:T(8,128)S(1)}, f32[1,4,8,128,128]{4,3,2,0,1:T(8,128)S(1)}, u32[]{:S(2)}, u32[]{:S(2)}) %collective-permute-start) | collective-permute-done | bytes 2097184 | tf_op jit(solution)/shard_map/ppermute | solution.py:12
  36.3 3.2 collective-permute-start.2
  39.6 6.9 %collective-permute-start.1 = (f32[4,4,1,128,128]{4,3,2,0,1:T(8,128)S(1)}, f32[4,4,1,128,128]{4,3,2,0,1:T(8,128)}, u32[]{:S(2)}, u32[]{:S(2)}) collective-permute-start(f32[4,4,1,128,128]{4,3,2,0,1:T(8,128)S(1)} %get-tuple-element.32), channel_id=1, source_target_pairs={{1,0},{2,1},{3,2},{4,3},{5,4},{6,5},{7,6},{8,7},{9,8},{10,9},{11,1... | collective-permute-start | bytes 3145736 | tf_op jit(solution)/shard_map/ppermute | solution.py:23
  47.7 20.2 %collective-permute-done.2 = f32[4,4,1,128,128]{4,3,2,0,1:T(8,128)S(1)} collective-permute-done((f32[4,4,1,128,128]{4,3,2,0,1:T(8,128)S(1)}, f32[4,4,1,128,128]{4,3,2,0,1:T(8,128)S(1)}, u32[]{:S(2)}, u32[]{:S(2)}) %collective-permute-start.2) | collective-permute-done | bytes 1048608 | tf_op jit(solution)/shard_map/ppermute | solution.py:22
  69.3 16.9 %fusion.5 = (f32[4,4,8,128,128]{4,3,2,0,1:T(8,128)}, f32[4,4,8,128,128]{4,3,2,0,1:T(8,128)}, f32[4,4,8,128,128]{4,3,2,0,1:T(8,128)}, f32[4,4,8,128,128]{4,3,2,0,1:T(8,128)}, f32[4,4,8,128,128]{4,3,2,0,1:T(8,128)}) fusion(f32[4,4,1,128,128]{4,3,2,0,1:T(8,128)} %collective-permute-done.1, f32[4,4,1,128,128]{4,3,2,0,1:T(8,128)S(1)} %collective-permute-done.2, ...), kind=kLoop, calls=%fused_computation.42 | loop fusion | flops 18874368 | bytes 52428800 | tf_op jit(solution)/shard_map/sub | solution.py:51
  86.2 4.2 %fusion.9 = f32[4,3,8,128,128]{4,3,2,0,1:T(8,128)S(1)} fusion(f32[4,4,8,128,128]{4,3,2,0,1:T(8,128)} %get-tuple-element.26, f32[4,4,8,128,128]{4,3,2,0,1:T(8,128)S(1)} %constant_dynamic-update-slice_fusion, f32[4,8,128,128]{3,2,1,0:T(8,128)S(1)} %slice_bitcast_fusion, f32[8,128,128]{2,1,0:T(8,128)S(1)} %multiply_divide_fusion, ...), kind=kLoop, calls=%fused_computation.63 | loop fusion | flops 12582912 | bytes 25165824 | tf_op jit(solution)/shard_map/mul | solution.py:64
  90.4 5.7 %fusion.22 = f32[4,1,8,128,128]{4,3,2,0,1:T(8,128)S(1)} fusion(bf16[4,8,128,128]{3,2,1,0:T(8,128)(2,1)S(1)} %copy-done.4, f32[4,4,8,128,128]{4,3,2,0,1:T(8,128)S(1)} %constant_dynamic-update-slice_fusion, f32[4,4,1,128,128]{4,3,2,0,1:T(8,128)} %collective-permute-done.1, f32[4,4,1,128,128]{4,3,2,0,1:T(8,128)} %copy-done.11, ...), kind=kLoop, calls=%fused_computation.85 | loop fusion | flops 9961472 | bytes 32505856 | tf_op jit(solution)/shard_map/broadcast_in_dim | solution.py:66
  97.7 25.6 %collective-permute-done.3 = f32[1,4,8,128,128]{4,3,2,0,1:T(8,128)S(1)} collective-permute-done((f32[1,4,8,128,128]{4,3,2,0,1:T(8,128)S(1)}, f32[1,4,8,128,128]{4,3,2,0,1:T(8,128)S(1)}, u32[]{:S(2)}, u32[]{:S(2)}) %collective-permute-start.3) | collective-permute-done | bytes 2097184 | tf_op jit(solution)/shard_map/ppermute | solution.py:12
  125.4 8.6 %collective-permute-start.4 = (f32[4,4,1,128,128]{4,3,2,0,1:T(8,128)S(1)}, f32[4,4,1,128,128]{4,3,2,0,1:T(8,128)}, u32[]{:S(2)}, u32[]{:S(2)}) collective-permute-start(f32[4,4,1,128,128]{4,3,2,0,1:T(8,128)S(1)} %get-tuple-element.25), channel_id=1, source_target_pairs={{1,0},{2,1},{3,2},{4,3},{5,4},{6,5},{7,6},{8,7},{9,8},{10,9},{11,1... | collective-permute-start | bytes 3145736 | tf_op jit(solution)/shard_map/ppermute | solution.py:23
  134.0 4.4 %pad_maximum_fusion = f32[4,4,8,128,128]{4,3,2,0,1:T(8,128)} fusion(f32[1,4,8,128,128]{4,3,2,0,1:T(8,128)S(1)} %collective-permute-done.3, f32[3,4,8,128,128]{4,3,2,0,1:T(8,128)S(1)} %fusion.7), kind=kLoop, calls=%fused_computation.16 | loop fusion | flops 2097152 | bytes 16777216 | tf_op jit(solution)/shard_map/concatenate | solution.py:75
  138.5 14.7 %collective-permute-done.5 = f32[4,4,1,128,128]{4,3,2,0,1:T(8,128)} collective-permute-done((f32[4,4,1,128,128]{4,3,2,0,1:T(8,128)S(1)}, f32[4,4,1,128,128]{4,3,2,0,1:T(8,128)}, u32[]{:S(2)}, u32[]{:S(2)}) %collective-permute-start.5) | collective-permute-done | bytes 1048608 | tf_op jit(solution)/shard_map/ppermute | solution.py:22
  154.8 46.7 %multiply_subtract_fusion.1 = (f32[4,4,8,128,128]{4,3,2,0,1:T(8,128)}, f32[4,4,8,128,128]{4,3,2,0,1:T(8,128)}, f32[4,4,8,128,128]{4,3,2,0,1:T(8,128)}, f32[4,4,8...) fusion(f32[1,4,8,128,128]{4,3,2,0,1:T(8,128)S(1)} %collective-p, ...), kind=kLoop, calls=%fused_computation.57 | loop fusion | flops 25165824 | bytes 77594624 | tf_op jit(solution)/shard_map/sub | solution.py:51
  201.6 7.7 %fusion.23 = (f32[4,1,8,128,128]{4,3,2,0,1:T(8,128)S(1)}, f32[4,8,128,128]{3,2,1,0:T(8,128)}) fusion(bf16[4,8,128,128]{3,2,1,0:T(8,128)(2,1)S(1)} %copy-done.4, f32[4,4,8,128,128]{4,3,2,0,1:T(8,128)} %get-tuple-element.22, f32[4,4,8,128,128]{4,3,2,0,1:T(8,128)} %get-tuple-element.23, f32[4,4,8,128,128]{4,3,2,0,1:T(8,128)} %get-tuple-element.13, ...), kind=kLoop, calls=%fused_computation.86 | loop fusion | flops 9437184 | bytes 34603008 | tf_op jit(solution)/shard_map/broadcast_in_dim | solution.py:66
  209.3 4.5 %fusion.11 = f32[4,3,8,128,128]{4,3,2,0,1:T(8,128)S(1)} fusion(f32[4,4,8,128,128]{4,3,2,0,1:T(8,128)} %get-tuple-element.11, f32[1,4,8,128,128]{4,3,2,0,1:T(8,128)S(1)} %collective-permute-done.3, f32[3,4,8,128,128]{4,3,2,0,1:T(8,128)S(1)} %fusion.7, f32[4,8,128,128]{3,2,1,0:T(8,128)} %get-tuple-element.10, f32[8,128,128]{2,1,0:T(8,128)S(1)} %copy-done.6, ...), kind=kLoop, calls=%fused_computation.65 | loop fusion | flops 14155776 | bytes 27262976 | tf_op jit(solution)/shard_map/mul | solution.py:64
  214.9 26.2 %collective-permute-done.6 = f32[1,4,8,128,128]{4,3,2,0,1:T(8,128)S(1)} collective-permute-done((f32[1,4,8,128,128]{4,3,2,0,1:T(8,128)S(1)}, f32[1,4,8,128,128]{4,3,2,0,1:T(8,128)S(1)}, u32[]{:S(2)}, u32[]{:S(2)}) %collective-permute-start.6) | collective-permute-done | bytes 2097184 | tf_op jit(solution)/shard_map/ppermute | solution.py:12
  243.1 8.4 %collective-permute-start.7 = (f32[4,4,1,128,128]{4,3,2,0,1:T(8,128)S(1)}, f32[4,4,1,128,128]{4,3,2,0,1:T(8,128)}, u32[]{:S(2)}, u32[]{:S(2)}) collective-permute-start(f32[4,4,1,128,128]{4,3,2,0,1:T(8,128)S(1)} %get-tuple-element.19), channel_id=1, source_target_pairs={{1,0},{2,1},{3,2},{4,3},{5,4},{6,5},{7,6},{8,7},{9,8},{10,9},{11,1... | collective-permute-start | bytes 3145736 | tf_op jit(solution)/shard_map/ppermute | solution.py:23
  251.5 4.4 %pad_maximum_fusion.1 = f32[4,4,8,128,128]{4,3,2,0,1:T(8,128)} fusion(f32[1,4,8,128,128]{4,3,2,0,1:T(8,128)S(1)} %collective-permute-done.6, f32[3,4,8,128,128]{4,3,2,0,1:T(8,128)S(1)} %fusion.6), kind=kLoop, calls=%fused_computation.21 | loop fusion | flops 2097152 | bytes 16777216 | tf_op jit(solution)/shard_map/concatenate | solution.py:75
  255.9 16.8 %collective-permute-done.8 = f32[4,4,1,128,128]{4,3,2,0,1:T(8,128)} collective-permute-done((f32[4,4,1,128,128]{4,3,2,0,1:T(8,128)S(1)}, f32[4,4,1,128,128]{4,3,2,0,1:T(8,128)}, u32[]{:S(2)}, u32[]{:S(2)}) %collective-permute-start.8) | collective-permute-done | bytes 1048608 | tf_op jit(solution)/shard_map/ppermute | solution.py:22
  274.2 46.7 %multiply_subtract_fusion = (f32[4,4,8,128,128]{4,3,2,0,1:T(8,128)}, f32[4,4,8,128,128]{4,3,2,0,1:T(8,128)}, f32[4,4,8,128,128]{4,3,2,0,1:T(8,128)}, f32[4,4,8,1...) fusion(f32[1,4,8,128,128]{4,3,2,0,1:T(8,128)S(1)} %collective-p, ...), kind=kLoop, calls=%fused_computation.56 | loop fusion | flops 25165824 | bytes 77594624 | tf_op jit(solution)/shard_map/sub | solution.py:51
  321.0 8.1 %fusion.24 = (f32[4,1,8,128,128]{4,3,2,1,0:T(8,128)}, f32[4,8,128,128]{3,2,1,0:T(8,128)}) fusion(bf16[4,8,128,128]{3,2,1,0:T(8,128)(2,1)S(1)} %copy-done.4, f32[4,4,8,128,128]{4,3,2,0,1:T(8,128)} %get-tuple-element.16, f32[4,4,8,128,128]{4,3,2,0,1:T(8,128)} %get-tuple-element.17, f32[4,4,8,128,128]{4,3,2,0,1:T(8,128)} %get-tuple-element.8, ...), kind=kLoop, calls=%fused_computation.87 | loop fusion | flops 9437184 | bytes 34603008 | tf_op jit(solution)/shard_map/broadcast_in_dim | solution.py:66
  330.3 7.3 %multiply_reduce_fusion = (f32[8,128,128]{2,1,0:T(8,128)}, f32[4,3,8,128,128]{4,3,2,0,1:T(8,128)}) fusion(bf16[4,3,8,128,128]{4,3,2,1,0:T(8,128)(2,1)} %param.8, bf16[4,3,8,128,128]{4,3,2,1,0:T(8,128)(2,1)} %param.9, f32[4,8,128,128]{3,2,1,0:T(8,128)} %get-tuple-element.5, f32[8,128,128]{2,1,0:T(8,128)S(1)} %copy-done.7, ...), kind=kLoop, calls=%fused_computation.80 | loop fusion | flops 18743296 | bytes 30932992 | tf_op jit(solution)/shard_map/reduce_sum | solution.py:78
  337.7 8.0 %pad_maximum_fusion.12 = f32[4,4,8,128,128]{4,3,2,1,0:T(8,128)} fusion(f32[4,1,8,128,128]{4,3,2,1,0:T(8,128)} %get-tuple-element.4, f32[4,3,8,128,128]{4,3,2,0,1:T(8,128)} %get-tuple-element.3), kind=kLoop, calls=%fused_computation.55 | loop fusion | flops 2097152 | bytes 16777216 | tf_op jit(solution)/shard_map/concatenate | solution.py:66
  345.7 33.5 %all-reduce.5.cloned.1.call-done = f32[8,128,128]{2,1,0:T(8,128)} async-done(((f32[8,128,128]{2,1,0:T(8,128)}), f32[8,128,128]{2,1,0:T(8,128)}) %all-reduce.5.cloned.1.call-update) | async-done | bytes 524304 | tf_op jit(solution)/shard_map/psum | solution.py:79
  (58 shorter events, 18.7 us)
Async XLA Ops:
  7.2 372.1 %all-reduce.5.cloned.1.call-start = ((), (), s32[]{:S(2)}) async-start(), calls=%async_computation | async-start | bytes 1048576 | tf_op jit(solution)/shard_map/psum | solution.py:79
  8.9 27.0 %collective-permute-start = (f32[1,4,8,128,128]{4,3,2,0,1:T(8,128)S(1)}, f32[1,4,8,128,128]{4,3,2,0,1:T(8,128)S(1)}, u32[]{:S(2)}, u32[]{:S(2)}) collective-permute-start(f32[1,4,8,128,128]{4,3,2,0,1:T(8,128)S(1)} %slice_bitcast_fusion.1), channel_id=1, source_target_pairs={{32,0},{64,32},{96,64},{0,96},{33,1},{65,33},{97,65},{1,97},{34,2}... | collective-permute-start | bytes 6291464 | tf_op jit(solution)/shard_map/ppermute | solution.py:12
  13.2 33.2 %copy-start.12 = (f32[8,128,128]{2,1,0:T(8,128)S(1)}, f32[8,128,128]{2,1,0:T(8,128)}, u32[]{:S(2)}) copy-start(f32[8,128,128]{2,1,0:T(8,128)} %param.11) | copy-start | bytes 1572868
  13.3 33.2 %copy-start.14 = (s32[8,128,128]{2,1,0:T(8,128)S(1)}, s32[8,128,128]{2,1,0:T(8,128)}, u32[]{:S(2)}) copy-start(s32[8,128,128]{2,1,0:T(8,128)} %param.12) | copy-start | bytes 1572868
  13.3 33.4 %copy-start.16 = (s32[8,128,128]{2,1,0:T(8,128)S(1)}, s32[8,128,128]{2,1,0:T(8,128)}, u32[]{:S(2)}) copy-start(s32[8,128,128]{2,1,0:T(8,128)} %param.13) | copy-start | bytes 1572868
  13.3 33.4 %copy-start.3 = (bf16[4,3,8,128,128]{4,3,2,1,0:T(8,128)(2,1)S(1)}, bf16[4,3,8,128,128]{4,3,2,1,0:T(8,128)(2,1)}, u32[]{:S(2)}) copy-start(bf16[4,3,8,128,128]{4,3,2,1,0:T(8,128)(2,1)} %param.8) | copy-start | bytes 9437188
  36.3 31.6 %collective-permute-start.2 = (f32[4,4,1,128,128]{4,3,2,0,1:T(8,128)S(1)}, f32[4,4,1,128,128]{4,3,2,0,1:T(8,128)S(1)}, u32[]{:S(2)}, u32[]{:S(2)}) collective-permute-start(f32[4,4,1,128,128]{4,3,2,0,1:T(8,128)S(1)} %get-tuple-element.31), channel_id=1, source_target_pairs={{0,1},{1,2},{2,3},{3,4},{4,5},{5,6},{6,7},{7,8},{8,9},{9,10},{10,1... | collective-permute-start | bytes 3145736 | tf_op jit(solution)/shard_map/ppermute | solution.py:22
  39.6 29.7 %collective-permute-start.1 = (f32[4,4,1,128,128]{4,3,2,0,1:T(8,128)S(1)}, f32[4,4,1,128,128]{4,3,2,0,1:T(8,128)}, u32[]{:S(2)}, u32[]{:S(2)}) collective-permute-start(f32[4,4,1,128,128]{4,3,2,0,1:T(8,128)S(1)} %get-tuple-element.32), channel_id=1, source_target_pairs={{1,0},{2,1},{3,2},{4,3},{5,4},{6,5},{7,6},{8,7},{9,8},{10,9},{11,1... | collective-permute-start | bytes 3145736 | tf_op jit(solution)/shard_map/ppermute | solution.py:23
  46.6 39.5 %copy-start.5 = (f32[8,128,128]{2,1,0:T(8,128)}, f32[8,128,128]{2,1,0:T(8,128)S(1)}, u32[]{:S(2)}) copy-start(f32[8,128,128]{2,1,0:T(8,128)S(1)} %multiply_divide_fusion) | copy-start | bytes 1572868
  46.7 39.4 %copy-start.8 = (f32[8,128,128]{2,1,0:T(8,128)}, f32[8,128,128]{2,1,0:T(8,128)S(1)}, u32[]{:S(2)}) copy-start(f32[8,128,128]{2,1,0:T(8,128)S(1)} %subtract_convert_fusion) | copy-start | bytes 1572868
  47.7 38.4 %copy-start.1 = (bf16[4,3,8,128,128]{4,3,2,1,0:T(8,128)(2,1)S(1)}, bf16[4,3,8,128,128]{4,3,2,1,0:T(8,128)(2,1)}, u32[]{:S(2)}) copy-start(bf16[4,3,8,128,128]{4,3,2,1,0:T(8,128)(2,1)} %param.9) | copy-start | bytes 9437188
  67.9 18.2 %copy-start.11 = (f32[4,4,1,128,128]{4,3,2,0,1:T(8,128)}, f32[4,4,1,128,128]{4,3,2,0,1:T(8,128)S(1)}, u32[]{:S(2)}) copy-start(f32[4,4,1,128,128]{4,3,2,0,1:T(8,128)S(1)} %collective-permute-done.2) | copy-start | bytes 3145732
  96.3 27.0 %collective-permute-start.3 = (f32[1,4,8,128,128]{4,3,2,0,1:T(8,128)S(1)}, f32[1,4,8,128,128]{4,3,2,0,1:T(8,128)S(1)}, u32[]{:S(2)}, u32[]{:S(2)}) collective-permute-start(f32[1,4,8,128,128]{4,3,2,0,1:T(8,128)S(1)} %pad_maximum_fusion.14), channel_id=1, source_target_pairs={{32,0},{64,32},{96,64},{0,96},{33,1},{65,33},{97,65},{1,97},{34,2}... | collective-permute-start | bytes 6291464 | tf_op jit(solution)/shard_map/ppermute | solution.py:12
  123.5 29.7 %collective-permute-start.5 = (f32[4,4,1,128,128]{4,3,2,0,1:T(8,128)S(1)}, f32[4,4,1,128,128]{4,3,2,0,1:T(8,128)}, u32[]{:S(2)}, u32[]{:S(2)}) collective-permute-start(f32[4,4,1,128,128]{4,3,2,0,1:T(8,128)S(1)} %get-tuple-element.24), channel_id=1, source_target_pairs={{0,1},{1,2},{2,3},{3,4},{4,5},{5,6},{6,7},{7,8},{8,9},{9,10},{10,1... | collective-permute-start | bytes 3145736 | tf_op jit(solution)/shard_map/ppermute | solution.py:22
  125.4 29.4 %collective-permute-start.4 = (f32[4,4,1,128,128]{4,3,2,0,1:T(8,128)S(1)}, f32[4,4,1,128,128]{4,3,2,0,1:T(8,128)}, u32[]{:S(2)}, u32[]{:S(2)}) collective-permute-start(f32[4,4,1,128,128]{4,3,2,0,1:T(8,128)S(1)} %get-tuple-element.25), channel_id=1, source_target_pairs={{1,0},{2,1},{3,2},{4,3},{5,4},{6,5},{7,6},{8,7},{9,8},{10,9},{11,1... | collective-permute-start | bytes 3145736 | tf_op jit(solution)/shard_map/ppermute | solution.py:23
  201.6 7.7 %copy-start.2 = (bf16[4,3,8,128,128]{4,3,2,1,0:T(8,128)(2,1)S(1)}, bf16[4,3,8,128,128]{4,3,2,1,0:T(8,128)(2,1)}, u32[]{:S(2)}) copy-start(bf16[4,3,8,128,128]{4,3,2,1,0:T(8,128)(2,1)} %param.9) | copy-start | bytes 9437188
  214.0 27.0 %collective-permute-start.6 = (f32[1,4,8,128,128]{4,3,2,0,1:T(8,128)S(1)}, f32[1,4,8,128,128]{4,3,2,0,1:T(8,128)S(1)}, u32[]{:S(2)}, u32[]{:S(2)}) collective-permute-start(f32[1,4,8,128,128]{4,3,2,0,1:T(8,128)S(1)} %pad_maximum_fusion.13), channel_id=1, source_target_pairs={{32,0},{64,32},{96,64},{0,96},{33,1},{65,33},{97,65},{1,97},{34,2}... | collective-permute-start | bytes 6291464 | tf_op jit(solution)/shard_map/ppermute | solution.py:12
  241.2 31.5 %collective-permute-start.8 = (f32[4,4,1,128,128]{4,3,2,0,1:T(8,128)S(1)}, f32[4,4,1,128,128]{4,3,2,0,1:T(8,128)}, u32[]{:S(2)}, u32[]{:S(2)}) collective-permute-start(f32[4,4,1,128,128]{4,3,2,0,1:T(8,128)S(1)} %get-tuple-element.18), channel_id=1, source_target_pairs={{0,1},{1,2},{2,3},{3,4},{4,5},{5,6},{6,7},{7,8},{8,9},{9,10},{10,1... | collective-permute-start | bytes 3145736 | tf_op jit(solution)/shard_map/ppermute | solution.py:22
  243.1 31.1 %collective-permute-start.7 = (f32[4,4,1,128,128]{4,3,2,0,1:T(8,128)S(1)}, f32[4,4,1,128,128]{4,3,2,0,1:T(8,128)}, u32[]{:S(2)}, u32[]{:S(2)}) collective-permute-start(f32[4,4,1,128,128]{4,3,2,0,1:T(8,128)S(1)} %get-tuple-element.19), channel_id=1, source_target_pairs={{1,0},{2,1},{3,2},{4,3},{5,4},{6,5},{7,6},{8,7},{9,8},{10,9},{11,1... | collective-permute-start | bytes 3145736 | tf_op jit(solution)/shard_map/ppermute | solution.py:23
  320.9 9.2 %copy-start = (f32[4,4,8,128,128]{4,3,2,0,1:T(8,128)S(1)}, f32[4,4,8,128,128]{4,3,2,0,1:T(8,128)}, u32[]{:S(2)}) copy-start(f32[4,4,8,128,128]{4,3,2,0,1:T(8,128)} %get-tuple-element.6) | copy-start | bytes 25165828
  321.0 9.2 %copy-start.7 = (f32[8,128,128]{2,1,0:T(8,128)S(1)}, f32[8,128,128]{2,1,0:T(8,128)}, u32[]{:S(2)}) copy-start(f32[8,128,128]{2,1,0:T(8,128)} %copy-done.5) | copy-start | bytes 1572868
  321.0 9.3 %copy-start.10 = (f32[8,128,128]{2,1,0:T(8,128)S(1)}, f32[8,128,128]{2,1,0:T(8,128)}, u32[]{:S(2)}) copy-start(f32[8,128,128]{2,1,0:T(8,128)} %copy-done.8) | copy-start | bytes 1572868
  337.6 41.6 %copy-start.13 = (f32[8,128,128]{2,1,0:T(8,128)S(1)}, f32[8,128,128]{2,1,0:T(8,128)}, u32[]{:S(2)}) copy-start(f32[8,128,128]{2,1,0:T(8,128)} %param.11) | copy-start | bytes 1572868
  337.7 41.6 %copy-start.15 = (s32[8,128,128]{2,1,0:T(8,128)S(1)}, s32[8,128,128]{2,1,0:T(8,128)}, u32[]{:S(2)}) copy-start(s32[8,128,128]{2,1,0:T(8,128)} %param.12) | copy-start | bytes 1572868
  (3 other events, 19.6 us)
Sparse Core Ops, SparseCore 0:
  337.8 41.4 all-reduce.4
where the time goes:
time: 390 us; the launch traced here: 388 us
  other arithmetic  170 us (44%)
  waiting for transfers between devices  164 us (42%)
  starting transfers between devices  32.3 us (8%)
  between operations  14.4 us (4%)
  local copies, waits for them, and re-layouts  7.13 us (2%)
    sub x3, other arithmetic, advance(): laplace = upper + lower + left + right + below + above - 6.0 * center  110 us
    ppermute x3, waiting for transfers between devices, passed_along(): return lax.ppermute(block, axis, route)  74.5 us
    ppermute x3, waiting for transfers between devices, padded_2(): before = lax.ppermute(last, axis, up)  51.7 us
    psum x1, waiting for transfers between devices, on_device(): summed = lax.psum(terms, 'phase')  33.5 us
    ppermute x3, starting transfers between devices, padded_2(): after = lax.ppermute(first, axis, down)  23.8 us
    broadcast_in_dim x3, other arithmetic, advance(): return jnp.concatenate([mom_new, jnp.expand_dims(heat_new, -4)], axis=-4)  21.4 us
    concatenate x5, other arithmetic, advance(): return jnp.concatenate([mom_new, jnp.expand_dims(heat_new, -4)], axis=-4)  10 us
    concatenate x4, other arithmetic, on_device(): later = jnp.concatenate([state[1:], first], axis=0)  9.09 us
  transfers between devices with their start and end apart: 10, of which 10 were waited for; matrix products, arithmetic and copies ran while one was open for 6% of the time, Pallas kernels for 0%

commit v1 on v0

v1 whole, which is shorter than its diff:
```python
import functools

import jax
import jax.numpy as jnp
from jax import lax
from jax.experimental import pallas as pl
from jax.experimental.pallas import tpu as pltpu
from jax.sharding import PartitionSpec as P

F32 = jnp.float32
PAD = 8
BLOCK = 32
TOP = 32767.0
MESH = pl.DeviceIdType.MESH


def rho_of(density, kind):
    return jnp.where(kind == 0, density, jnp.where(kind == 2, 1.0, 0.0))


def kernel(
    tiles, adj, vel, grad, heat, density, kind, inlet, out, sens,
    state, fin, v_buf, g_buf, w_buf, d_buf, k_buf, i_buf, cen, nbr, keep, acc, half, part, whole,
    xs_q, xs_s, xr_q, xr_s, hs_q, hs_s, hr_q, hr_s,
    load_sem, out_sem, x_send, x_recv, h_send, h_recv, s_send, s_recv,
):
    ny, nx, nz = d_buf.shape
    group, tile = lax.axis_index("phase"), lax.axis_index("tile")
    core = lax.rem(group, 2)
    before, after, across = (lax.rem(group + n, 4) for n in (3, 1, 2))
    partner = group + 1 - 2 * core
    has_down, has_up = tile > 0, tile < tiles - 1
    body = pl.ds(PAD, nx)

    loads = {}

    def load(name, number, src, dst):
        loads[name] = pltpu.make_async_copy(src, dst, load_sem.at[number])
        loads[name].start()

    for t in range(4):
        load(f"s{t}", t, adj.at[t], state.at[t, :, pl.ds(1, ny), body, :])
    load("density", 4, density, d_buf)
    load("kind", 5, kind, k_buf)
    load("inlet", 6, inlet, i_buf)
    for t in (0, 1, 2, 3):
        load(f"v{t}", 7 + 3 * t, vel.at[t], v_buf.at[t])
        load(f"g{t}", 8 + 3 * t, grad.at[t], g_buf.at[t])
        load(f"w{t}", 9 + 3 * t, heat.at[t], w_buf.at[t])

    edge = jnp.zeros((PAD, nz), F32)

    def clear(y, carry):
        for slot in range(state.shape[0]):
            for c in range(4):
                state[slot, c, y, 0:PAD, :] = edge
                state[slot, c, y, PAD + nx : 2 * PAD + nx, :] = edge
        return carry

    lax.fori_loop(0, ny + 2, clear, 0)

    barrier = pltpu.get_barrier_semaphore()
    for other in (before, after, across):
        pl.semaphore_signal(barrier, 1, device_id=(other, tile), device_id_type=MESH)

    @pl.when(has_down)
    def _():
        pl.semaphore_signal(barrier, 1, device_id=(group, tile - 1), device_id_type=MESH)

    @pl.when(has_up)
    def _():
        pl.semaphore_signal(barrier, 1, device_id=(group, tile + 1), device_id_type=MESH)

    pl.semaphore_wait(barrier, 3 + has_down.astype(jnp.int32) + has_up.astype(jnp.int32))

    def encode(slot, y, q, s):
        for c in range(4):
            v = state[slot, c, y + 1, PAD : PAD + nx, :]
            top = jnp.maximum(jnp.max(jnp.abs(v), axis=0, keepdims=True), 1e-30)
            q[c] = jnp.round(v * (TOP / top)).astype(jnp.int32).astype(jnp.int16)
            scale = top * (1.0 / TOP)
            s[c : c + 1, :] = scale
            s[c + 4 : c + 5, :] = scale

    def decode(q, s, slot, row):
        for c in range(4):
            code = q[c].astype(jnp.int32).astype(F32)
            state[slot, c, row, PAD : PAD + nx, :] = code * s[c : c + 1, :]

    def crossing(u, y):
        return [
            pltpu.make_async_remote_copy(
                a.at[u, y], b.at[u, y], x_send.at[u, y, n], x_recv.at[u, y, n],
                device_id=(before, tile), device_id_type=MESH,
            )
            for n, (a, b) in enumerate(((xs_q, xr_q), (xs_s, xr_s)))
        ]

    def cross(u, slot, y):
        encode(slot, y, xs_q.at[u, y], xs_s.at[u, y])
        for copy in crossing(u, y):
            copy.start()

    def halo(u, side, q, s):
        other = tile + 1 - 2 * side
        return [
            pltpu.make_async_remote_copy(
                a, b.at[u, side], h_send.at[u, side, n], h_recv.at[u, side, n],
                device_id=(group, other), device_id_type=MESH,
            )
            for n, (a, b) in enumerate(((q, hr_q), (s, hr_s)))
        ]

    def offer(u, slot):
        for side, there, y in ((0, has_up, ny - 1), (1, has_down, 0)):

            @pl.when(there)
            def _():
                encode(slot, y, hs_q.at[u, side], hs_s.at[u, side])
                for copy in halo(u, side, hs_q.at[u, side], hs_s.at[u, side]):
                    copy.start()

    def relay(u, x):
        for side, there, y in ((0, has_up, ny - 1), (1, has_down, 0)):
            for copy in crossing(x, y):
                copy.wait_recv()

            @pl.when(there)
            def _():
                for copy in halo(u, side, xr_q.at[x, y], xr_s.at[x, y]):
                    copy.start()

    def take_halo(u, slot):
        for side, there, row in ((0, has_down, 0), (1, has_up, ny + 1)):

            @pl.when(there)
            def _():
                for copy in halo(u, side, hs_q.at[u, side], hs_s.at[u, side]):
                    copy.wait_recv()
                decode(hr_q.at[u, side], hr_s.at[u, side], slot, row)

            @pl.when(jnp.logical_not(there))
            def _():
                for c in range(4):
                    state[slot, c, row, PAD : PAD + nx, :] = jnp.zeros((nx, nz), F32)

    def take_plane(x, slot, y, wait):
        if wait:
            for copy in crossing(x, y):
                copy.wait_recv()
        decode(xr_q.at[x, y], xr_s.at[x, y], slot, y + 1)

    lane = lax.broadcasted_iota(jnp.int32, (BLOCK, nz), 1)
    not_first, not_last = lane > 0, lane < nz - 1

    def plane(slot, t, y, target, total):
        for x0 in range(0, nx, BLOCK):
            rows = slice(PAD + x0, PAD + x0 + BLOCK)
            left = slice(PAD + x0 - 1, PAD + x0 + BLOCK - 1)
            right = slice(PAD + x0 + 1, PAD + x0 + BLOCK + 1)
            here = slice(x0, x0 + BLOCK)

            def around(c):
                mid = state[slot, c, y + 1, rows, :]
                below = jnp.where(not_first, pltpu.roll(mid, 1, 1), 0.0)
                above = jnp.where(not_last, pltpu.roll(mid, nz - 1, 1), 0.0)
                return (
                    mid, state[slot, c, y + 1, left, :], state[slot, c, y + 1, right, :],
                    state[slot, c, y, rows, :], state[slot, c, y + 2, rows, :], below, above,
                )

            h, xl, xr, yl, yu, zl, zr = around(3)
            speed = [v_buf[t, c, y, here, :].astype(F32) for c in range(3)]
            turn = speed[0] * (xr - xl) + speed[1] * (yu - yl) + speed[2] * (zr - zl)
            ring = (xl + xr) + (yl + yu) + (zl + zr)
            h_new = 0.28 * h + 0.12 * ring + 0.1 * turn + w_buf[t, y, here, :].astype(F32)
            put(target, 3, y, x0, h_new)
            kh = keep[y, here, :] * h
            a, b = cen[y, here, :], nbr[y, here, :]
            term = None
            for c in range(3):
                m, xl, xr, yl, yu, zl, zr = around(c)
                ring = (xl + xr) + (yl + yu) + (zl + zr)
                new = a * m + b * ring - kh * g_buf[t, c, y, here, :].astype(F32)
                put(target, c, y, x0, new)
                if total is not None:
                    term = speed[c] * new if term is None else term + speed[c] * new
            if total == "set":
                acc[y, here, :] = term
            elif total == "add":
                acc[y, here, :] = acc[y, here, :] + term

    def put(target, c, y, x0, value):
        kind_of, number = target
        if kind_of == "fin":
            fin[number, c, y, x0 : x0 + BLOCK, :] = value
        else:
            state[number, c, y + 1, PAD + x0 : PAD + x0 + BLOCK, :] = value

    def out_copy(t, y):
        return pltpu.make_async_copy(fin.at[t, :, y], out.at[t, :, y], out_sem.at[t, y])

    def chain(slot, t, target, halo_out=None, cross_out=None, total=None):
        def one(i, carry):
            y = lax.rem(i + ny - 1, ny)
            plane(slot, t, y, target, total)
            if cross_out is not None:
                cross(cross_out, target[1], y)
            if target[0] == "fin":
                out_copy(t, y).start()
            if halo_out is not None:

                @pl.when(i == 1)
                def _():
                    offer(halo_out, target[1])

            return carry

        lax.fori_loop(0, ny, one, 0)

    def take_crossing(x, slot):
        def one(i, carry):
            take_plane(x, slot, i, True)
            return carry

        lax.fori_loop(1, ny - 1, one, 0)
        take_plane(x, slot, 0, False)
        take_plane(x, slot, ny - 1, False)

    loads["s0"].wait()

    def first(i, carry):
        cross(0, 0, lax.rem(i + ny - 1, ny))
        return carry

    lax.fori_loop(0, ny, first, 0)
    for t in (1, 2, 3):
        loads[f"s{t}"].wait()
        offer(t - 1, t)

    for name in ("density", "kind", "inlet"):
        loads[name].wait()

    def prepare(y, carry):
        rho = rho_of(d_buf[y], k_buf[y])
        under = 1.0 / (0.5 + rho)
        open_ = (1 - i_buf[y]).astype(F32)
        keep[y] = open_
        nbr[y] = 0.12 * open_
        cen[y] = open_ * (0.28 - 0.25 * (1.0 - rho) * under)
        d_buf[y] = jnp.where(k_buf[y] == 0, -0.375 * under * under, 0.0)
        return carry

    lax.fori_loop(0, ny, prepare, 0)

    def ready(t):
        for n in "vgw":
            loads[f"{n}{t}"].wait()

    S = "state"
    ready(0)
    take_halo(0, 1)
    chain(1, 0, (S, 4), cross_out=1)
    ready(1)
    take_halo(1, 2)
    chain(2, 1, (S, 5), halo_out=3)
    relay(4, 0)
    ready(2)
    take_halo(2, 3)
    chain(3, 2, (S, 1), halo_out=5)
    take_halo(3, 5)
    chain(5, 0, (S, 4), cross_out=2)
    ready(3)
    take_crossing(0, 0)
    take_halo(4, 0)
    chain(0, 3, (S, 3), halo_out=6)
    take_halo(5, 1)
    chain(1, 1, (S, 2), halo_out=7)
    relay(8, 1)
    take_halo(6, 3)
    chain(3, 2, (S, 1), halo_out=9)
    take_halo(7, 2)
    chain(2, 0, ("fin", 0), total="set")
    take_halo(9, 1)
    chain(1, 1, ("fin", 1), total="add")
    take_crossing(1, 0)
    take_halo(8, 0)
    chain(0, 3, (S, 4), halo_out=10)
    relay(11, 2)
    take_halo(10, 4)
    chain(4, 2, ("fin", 2), total="add")
    take_crossing(2, 5)
    take_halo(11, 5)
    chain(5, 3, ("fin", 3), total="add")

    mine, theirs = pl.ds(core * (ny // 2), ny // 2), pl.ds((1 - core) * (ny // 2), ny // 2)

    def send(n, src, dst, other):
        return pltpu.make_async_remote_copy(
            src, dst, s_send.at[n], s_recv.at[n], device_id=(other, tile), device_id_type=MESH
        )

    swap = send(0, acc.at[theirs], part.at[0], partner)
    swap.start()
    swap.wait_recv()
    half[...] = acc[mine] + part[0]
    far = send(1, half, part.at[1], across)
    far.start()
    far.wait_recv()
    whole[mine] = half[...] + part[1]
    back = send(2, whole.at[mine], whole.at[mine], partner)
    back.start()
    swap.wait_send()
    send(2, whole.at[theirs], whole.at[theirs], partner).wait_recv()
    far.wait_send()
    back.wait_send()
    acc[...] = d_buf[...] * whole[...]
    last = pltpu.make_async_copy(acc, sens, load_sem.at[0])
    last.start()

    def settle(y, carry):
        for u in range(3):
            for copy in crossing(u, y):
                copy.wait_send()
        for t in range(4):
            out_copy(t, y).wait()
        return carry

    lax.fori_loop(0, ny, settle, 0)
    for side, there in ((0, has_up), (1, has_down)):

        @pl.when(there)
        def _():
            for u in range(12):
                for copy in halo(u, side, hs_q.at[u, side], hs_s.at[u, side]):
                    copy.wait_send()

    last.wait()


def on_device(tiles, adjoint_in, velocity, temp_grad, heat_weight, density, cell_kind, inlet):
    phases, _, ny, nx, nz = adjoint_in.shape
    bf16, i16, i32 = jnp.bfloat16, jnp.int16, jnp.int32
    vmem, dma = pltpu.VMEM, pltpu.SemaphoreType.DMA
    return pl.pallas_call(
        functools.partial(kernel, tiles),
        out_shape=(
            jax.ShapeDtypeStruct(adjoint_in.shape, F32),
            jax.ShapeDtypeStruct(density.shape, F32),
        ),
        in_specs=[pl.BlockSpec(memory_space=pl.ANY)] * 7,
        out_specs=[pl.BlockSpec(memory_space=pl.ANY)] * 2,
        scratch_shapes=[
            vmem((6, 4, ny + 2, nx + 2 * PAD, nz), F32),
            vmem((phases, 4, ny, nx, nz), F32),
            vmem((phases, 3, ny, nx, nz), bf16),
            vmem((phases, 3, ny, nx, nz), bf16),
            vmem((phases, ny, nx, nz), bf16),
            vmem((ny, nx, nz), F32),
            vmem((ny, nx, nz), i32),
            vmem((ny, nx, nz), i32),
            vmem((ny, nx, nz), F32),
            vmem((ny, nx, nz), F32),
            vmem((ny, nx, nz), F32),
            vmem((ny, nx, nz), F32),
            vmem((ny // 2, nx, nz), F32),
            vmem((2, ny // 2, nx, nz), F32),
            vmem((ny, nx, nz), F32),
            vmem((3, ny, 4, nx, nz), i16),
            vmem((3, ny, 8, nz), F32),
            vmem((3, ny, 4, nx, nz), i16),
            vmem((3, ny, 8, nz), F32),
            vmem((12, 2, 4, nx, nz), i16),
            vmem((12, 2, 8, nz), F32),
            vmem((12, 2, 4, nx, nz), i16),
            vmem((12, 2, 8, nz), F32),
            dma((19,)),
            dma((phases, ny)),
            dma((3, ny, 2)),
            dma((3, ny, 2)),
            dma((12, 2, 2)),
            dma((12, 2, 2)),
            dma((3,)),
            dma((3,)),
        ],
        compiler_params=pltpu.CompilerParams(
            collective_id=0, has_side_effects=True, vmem_limit_bytes=60 * 2**20
        ),
    )(adjoint_in, velocity, temp_grad, heat_weight, density, cell_kind, inlet)


def solution(mesh):
    return jax.shard_map(
        functools.partial(on_device, mesh.shape["tile"]),
        mesh=mesh,
        in_specs=(
            P("phase", None, "tile", None, None),
            P("phase", None, "tile", None, None),
            P("phase", None, "tile", None, None),
            P("phase", "tile", None, None),
            P("tile", None, None),
            P("tile", None, None),
            P("tile", None, None),
        ),
        out_specs=(P("phase", None, "tile", None, None), P("tile", None, None)),
        check_vma=False,
    )
```

time: 390 us -> 117 us (0.30)
  other arithmetic: 170 us -> 0 us
  waiting for transfers between devices: 164 us -> 0 us
  Pallas kernels: 0 us -> 107 us
  starting transfers between devices: 32.3 us -> 0 us
  between operations: 14.4 us -> 0.65 us
    ppermute x9 -> x0, waiting for transfers between devices: 131 us -> none  [the longest x3 74.5 us: passed_along(): return lax.ppermute(block, axis, route)]
    sub x3 -> x0, other arithmetic: 110 us -> none  [advance(): laplace = upper + lower + left + right + below + above - 6.0 * center]
    pallas_call x0 -> x1, Pallas kernels: none -> 107 us  [on_device(): pl.pallas_call(functools.partial(kernel, tiles), out_shape=(jax.ShapeDtyp...]
    psum x1 -> x0, waiting for transfers between devices: 33.5 us -> none  [on_device(): summed = lax.psum(terms, 'phase')]
    ppermute x9 -> x0, starting transfers between devices: 32.3 us -> none  [the longest x3 23.8 us: padded_2(): after = lax.ppermute(first, axis, down)]
    broadcast_in_dim x3 -> x0, other arithmetic: 21.4 us -> none  [advance(): return jnp.concatenate([mom_new, jnp.expand_dims(heat_new, -4)], axis=-4)]
    concatenate x9 -> x0, other arithmetic: 19.1 us -> none  [the longest x5 10 us: advance(): return jnp.concatenate([mom_new, jnp.expand_dims(heat_new, -4)], axis=-4)]
    mul x3 -> x0, other arithmetic: 10.8 us -> none  [the longest x2 8.76 us: advance(): keep * (momentum + 0.12 * laplace[..., 0:3, :, :, :] - penalty * momentum...]
  transfers between devices with their start and end apart: 10 -> 0, of which waited for: 10 -> 0; matrix products, arithmetic and copies ran while one was open for 6% -> 0% of each run, Pallas kernels for 0% -> 0%
where the time goes in v1:
time: 117 us
  Pallas kernels  107 us (91%)
  local copies, waits for them, and re-layouts  8.74 us (7%)
    pallas_call x1, Pallas kernels, on_device(): pl.pallas_call(functools.partial(kernel, tiles), out_shape=(jax.ShapeDtyp...  107 us
    unnamed x4, local copies, waits for them, and re-layouts  8.74 us

profile of v1, /device:TPU:3, one launch (start us, length us, event | category | flops | bytes accessed | tf_op | source)
XLA Modules:
  0.0 116.8 jit_solution(17665644882623377887)
XLA Ops:
  0.6 107.4 %shard_map.86 = (f32[4,4,8,128,128]{4,3,2,1,0:T(8,128)}, f32[8,128,128]{2,1,0:T(8,128)}) custom-call(f32[4,4,8,128,128]{4,3,2,1,0:T(8,128)} %adj.1, bf16[4,3,8,128,128]{4,3,2,1,0:T(8,128)(2,1)} %vel.1, bf16[4,3,8,128,128]{4,3,2,1,0:T(8,128)(2,1)} %grad.1, bf16[4,8,128,128]{3,2,1,0:T(8,128)(2,1)} %heat.1, f32[8,128,128]{2,1,0:T(8,128)} %density.1, ...), custom_call_target="tpu_custom_call" | custom-call | tf_op jit(solution)/shard_map/pallas_call | solution.py:345
  108.1 0.0 copy-start
  108.1 7.9 %copy.11 = f32[4,4,8,128,128]{4,3,2,1,0:T(8,128)} copy(f32[4,4,8,128,128]{4,3,2,1,0:T(8,128)} %get-tuple-element.4) | data formatting | bytes 16777216
  116.0 0.0 copy-done
  116.0 0.8 copy.12
Async XLA Ops:
  108.1 8.0 %copy-start = (f32[8,128,128]{2,1,0:T(8,128)S(1)}, f32[8,128,128]{2,1,0:T(8,128)}, u32[]{:S(2)}) copy-start(f32[8,128,128]{2,1,0:T(8,128)} %get-tuple-element.5) | copy-start | bytes 1572868

commit v2 on v1

--- a/solution.py
+++ b/solution.py
@@ -20,13 +20,22 @@
 
 def kernel(
     tiles, adj, vel, grad, heat, density, kind, inlet, out, sens,
-    state, fin, v_buf, g_buf, w_buf, d_buf, k_buf, i_buf, cen, nbr, keep, acc, half, part, whole,
-    xs_q, xs_s, xr_q, xr_s, hs_q, hs_s, hr_q, hr_s,
-    load_sem, out_sem, x_send, x_recv, h_send, h_recv, s_send, s_recv,
+    state, fin, v_buf, g_buf, w_buf, d_buf, k_buf, i_buf, cen, nbr, keep, acc, half, near, far, whole,
+    xs_q, xs_s, xr_q, xr_s, hs_q, hs_s, hr_q, hr_s, via_q,
+    load_sem, out_sem, x_send, x_recv, h_send, h_recv, s_send, s_recv, via_send, via_recv,
 ):
     ny, nx, nz = d_buf.shape
     group, tile = lax.axis_index("phase"), lax.axis_index("tile")
     core = lax.rem(group, 2)
+    lower = 1 - tile // (tiles // 2)
+    place = lower * tile + (1 - lower) * (tiles - 1 - tile)
+    vias = (0, 3, 12)
+    via = (place == vias[0]) | (place == vias[1]) | (place == vias[2])
+    via_part = 1 + place // 3 - 2 * (place // 12)
+    meets = place == tiles // 2 - 1
+    lower_end, upper_end = tiles // 2 - 1, tiles // 2
+    via_from = lower * lower_end + (1 - lower) * upper_end
+    via_to = tiles - 1 - via_from
     before, after, across = (lax.rem(group + n, 4) for n in (3, 1, 2))
     partner = group + 1 - 2 * core
     has_down, has_up = tile > 0, tile < tiles - 1
@@ -38,15 +47,24 @@
         loads[name] = pltpu.make_async_copy(src, dst, load_sem.at[number])
         loads[name].start()
 
-    for t in range(4):
+    def load_state(t):
         load(f"s{t}", t, adj.at[t], state.at[t, :, pl.ds(1, ny), body, :])
+
+    def load_flow(t):
+        load(f"v{t}", 7 + 3 * t, vel.at[t], v_buf.at[t])
+        load(f"g{t}", 8 + 3 * t, grad.at[t], g_buf.at[t])
+        load(f"w{t}", 9 + 3 * t, heat.at[t], w_buf.at[t])
+
+    load_state(0)
+    load_state(1)
+    load_state(2)
     load("density", 4, density, d_buf)
     load("kind", 5, kind, k_buf)
     load("inlet", 6, inlet, i_buf)
-    for t in (0, 1, 2, 3):
-        load(f"v{t}", 7 + 3 * t, vel.at[t], v_buf.at[t])
-        load(f"g{t}", 8 + 3 * t, grad.at[t], g_buf.at[t])
-        load(f"w{t}", 9 + 3 * t, heat.at[t], w_buf.at[t])
+    load_flow(0)
+    load_state(3)
+    for t in (1, 2, 3):
+        load_flow(t)
 
     edge = jnp.zeros((PAD, nz), F32)
 
@@ -71,7 +89,18 @@
     def _():
         pl.semaphore_signal(barrier, 1, device_id=(group, tile + 1), device_id_type=MESH)
 
-    pl.semaphore_wait(barrier, 3 + has_down.astype(jnp.int32) + has_up.astype(jnp.int32))
+    @pl.when(via)
+    def _():
+        pl.semaphore_signal(barrier, 1, device_id=(group, via_from), device_id_type=MESH)
+
+    @pl.when(meets)
+    def _():
+        for v in vias:
+            other = (1 - lower) * v + lower * (tiles - 1 - v)
+            pl.semaphore_signal(barrier, 1, device_id=(group, other), device_id_type=MESH)
+
+    extra = via.astype(jnp.int32) + 3 * meets.astype(jnp.int32)
+    pl.semaphore_wait(barrier, 3 + has_down.astype(jnp.int32) + has_up.astype(jnp.int32) + extra)
 
     def encode(slot, y, q, s):
         for c in range(4):
@@ -96,10 +125,14 @@
             for n, (a, b) in enumerate(((xs_q, xr_q), (xs_s, xr_s)))
         ]
 
-    def cross(u, slot, y):
-        encode(slot, y, xs_q.at[u, y], xs_s.at[u, y])
+    order = iter([(u, (i + ny - 1) % ny) for u in range(3) for i in range(ny)])
+
+    def cross(u, y):
         for copy in crossing(u, y):
             copy.start()
+
+    def encode_crossing(u, slot, y):
+        encode(slot, y, xs_q.at[u, y], xs_s.at[u, y])
 
     def halo(u, side, q, s):
         other = tile + 1 - 2 * side
@@ -111,14 +144,51 @@
             for n, (a, b) in enumerate(((q, hr_q), (s, hr_s)))
         ]
 
+    def post(u, side, q, s):
+        number, scale = halo(u, side, q, s)
+        far_apart = tile == (lower_end, upper_end)[side]
+
+        @pl.when(jnp.logical_not(far_apart))
+        def _():
+            number.start()
+
+        @pl.when(far_apart)
+        def _():
+            pltpu.make_async_remote_copy(
+                q.at[0], hr_q.at[u, side, 0], h_send.at[u, side, 0], h_recv.at[u, side, 0],
+                device_id=(group, tile + 1 - 2 * side), device_id_type=MESH,
+            ).start()
+            for c, v in enumerate(vias, 1):
+                pltpu.make_async_remote_copy(
+                    q.at[c], via_q.at[u], h_send.at[u, side, 0], via_recv.at[u],
+                    device_id=(group, (v, tiles - 1 - v)[side]), device_id_type=MESH,
+                ).start()
+
+        scale.start()
+
+    def passed_on(u):
+        return pltpu.make_async_remote_copy(
+            via_q.at[u], hr_q.at[u, 1 - lower, via_part], via_send.at[u], h_recv.at[u, 1 - lower, 0],
+            device_id=(group, via_to), device_id_type=MESH,
+        )
+
+    def pass_on(*units):
+        @pl.when(via)
+        def _():
+            for u in units:
+                pltpu.make_async_remote_copy(
+                    via_q.at[u], via_q.at[u], via_send.at[u], via_recv.at[u],
+                    device_id=(group, via_to), device_id_type=MESH,
+                ).wait_recv()
+                passed_on(u).start()
+
     def offer(u, slot):
         for side, there, y in ((0, has_up, ny - 1), (1, has_down, 0)):
 
             @pl.when(there)
             def _():
                 encode(slot, y, hs_q.at[u, side], hs_s.at[u, side])
-                for copy in halo(u, side, hs_q.at[u, side], hs_s.at[u, side]):
-                    copy.start()
+                post(u, side, hs_q.at[u, side], hs_s.at[u, side])
 
     def relay(u, x):
         for side, there, y in ((0, has_up, ny - 1), (1, has_down, 0)):
@@ -127,8 +197,7 @@
 
             @pl.when(there)
             def _():
-                for copy in halo(u, side, xr_q.at[x, y], xr_s.at[x, y]):
-                    copy.start()
+                post(u, side, xr_q.at[x, y], xr_s.at[x, y])
 
     def take_halo(u, slot):
         for side, there, row in ((0, has_down, 0), (1, has_up, ny + 1)):
@@ -200,12 +269,14 @@
     def out_copy(t, y):
         return pltpu.make_async_copy(fin.at[t, :, y], out.at[t, :, y], out_sem.at[t, y])
 
-    def chain(slot, t, target, halo_out=None, cross_out=None, total=None):
+    def chain(slot, t, target, halo_out=None, cross_out=None, total=None, crosses=0):
+        due = [next(order) for _ in range(crosses)]
+
         def one(i, carry):
             y = lax.rem(i + ny - 1, ny)
             plane(slot, t, y, target, total)
             if cross_out is not None:
-                cross(cross_out, target[1], y)
+                encode_crossing(cross_out, target[1], y)
             if target[0] == "fin":
                 out_copy(t, y).start()
             if halo_out is not None:
@@ -213,6 +284,12 @@
                 @pl.when(i == 1)
                 def _():
                     offer(halo_out, target[1])
+
+            for n, (u, plane_of) in enumerate(due):
+
+                @pl.when(i == 2 + 2 * n)
+                def _(u=u, plane_of=plane_of):
+                    cross(u, plane_of)
 
             return carry
 
@@ -230,13 +307,16 @@
     loads["s0"].wait()
 
     def first(i, carry):
-        cross(0, 0, lax.rem(i + ny - 1, ny))
+        encode_crossing(0, 0, lax.rem(i + ny - 1, ny))
         return carry
 
     lax.fori_loop(0, ny, first, 0)
     for t in (1, 2, 3):
         loads[f"s{t}"].wait()
         offer(t - 1, t)
+        if t == 1:
+            cross(*next(order))
+            cross(*next(order))
 
     for name in ("density", "kind", "inlet"):
         loads[name].wait()
@@ -258,65 +338,121 @@
             loads[f"{n}{t}"].wait()
 
     S = "state"
+    pass_on(0, 1, 2)
     ready(0)
     take_halo(0, 1)
-    chain(1, 0, (S, 4), cross_out=1)
+    chain(1, 0, (S, 4), cross_out=1, crosses=3)
     ready(1)
     take_halo(1, 2)
-    chain(2, 1, (S, 5), halo_out=3)
+    chain(2, 1, (S, 5), halo_out=3, crosses=3)
+    pass_on(3)
     relay(4, 0)
     ready(2)
     take_halo(2, 3)
-    chain(3, 2, (S, 1), halo_out=5)
+    chain(3, 2, (S, 1), halo_out=5, crosses=3)
+    pass_on(4, 5)
     take_halo(3, 5)
-    chain(5, 0, (S, 4), cross_out=2)
+    chain(5, 0, (S, 4), cross_out=2, crosses=3)
     ready(3)
     take_crossing(0, 0)
     take_halo(4, 0)
-    chain(0, 3, (S, 3), halo_out=6)
+    chain(0, 3, (S, 3), halo_out=6, crosses=2)
+    pass_on(6)
     take_halo(5, 1)
-    chain(1, 1, (S, 2), halo_out=7)
+    chain(1, 1, (S, 2), halo_out=7, crosses=3)
+    pass_on(7)
     relay(8, 1)
     take_halo(6, 3)
-    chain(3, 2, (S, 1), halo_out=9)
+    chain(3, 2, (S, 1), halo_out=9, crosses=3)
+    pass_on(8, 9)
     take_halo(7, 2)
-    chain(2, 0, ("fin", 0), total="set")
+    chain(2, 0, ("fin", 0), total="set", crosses=2)
     take_halo(9, 1)
-    chain(1, 1, ("fin", 1), total="add")
+    chain(1, 1, ("fin", 1), total="add", crosses=0)
     take_crossing(1, 0)
     take_halo(8, 0)
-    chain(0, 3, (S, 4), halo_out=10)
+    chain(0, 3, (S, 4), halo_out=10, crosses=0)
+    pass_on(10)
     relay(11, 2)
     take_halo(10, 4)
-    chain(4, 2, ("fin", 2), total="add")
-    take_crossing(2, 5)
+    chain(4, 2, ("fin", 2), total="add", crosses=0)
+    pass_on(11)
+
+    def mine(k):
+        return 2 * k + core
+
+    def theirs(k):
+        return 2 * k + 1 - core
+
+    def send(n, k, src, dst, other):
+        return pltpu.make_async_remote_copy(
+            src, dst, s_send.at[n, k], s_recv.at[n, k], device_id=(other, tile), device_id_type=MESH
+        )
+
+    def to_partner(k):
+        return send(0, k, acc.at[theirs(k)], near.at[k], partner)
+
+    def to_other_chip(k):
+        return send(1, k, half.at[k], far.at[k], across)
+
+    def back(k, y):
+        return send(2, k, whole.at[y], whole.at[y], partner)
+
+    def sens_copy(y):
+        return pltpu.make_async_copy(whole.at[y], sens.at[y], out_sem.at[4, y])
+
+    def sum_chip(k):
+        to_partner(k).wait_recv()
+        half[k] = acc[mine(k)] + near[k]
+        to_other_chip(k).start()
+
+    def sum_all(k):
+        to_other_chip(k).wait_recv()
+        y = mine(k)
+        whole[y] = d_buf[y] * (half[k] + far[k])
+        back(k, y).start()
+        sens_copy(y).start()
+
     take_halo(11, 5)
-    chain(5, 3, ("fin", 3), total="add")
-
-    mine, theirs = pl.ds(core * (ny // 2), ny // 2), pl.ds((1 - core) * (ny // 2), ny // 2)
-
-    def send(n, src, dst, other):
-        return pltpu.make_async_remote_copy(
-            src, dst, s_send.at[n], s_recv.at[n], device_id=(other, tile), device_id_type=MESH
-        )
-
-    swap = send(0, acc.at[theirs], part.at[0], partner)
-    swap.start()
-    swap.wait_recv()
-    half[...] = acc[mine] + part[0]
-    far = send(1, half, part.at[1], across)
-    far.start()
-    far.wait_recv()
-    whole[mine] = half[...] + part[1]
-    back = send(2, whole.at[mine], whole.at[mine], partner)
-    back.start()
-    swap.wait_send()
-    send(2, whole.at[theirs], whole.at[theirs], partner).wait_recv()
-    far.wait_send()
-    back.wait_send()
-    acc[...] = d_buf[...] * whole[...]
-    last = pltpu.make_async_copy(acc, sens, load_sem.at[0])
-    last.start()
+    take_plane(2, 5, 0, False)
+    take_plane(2, 5, ny - 1, False)
+
+    def last_pair(k, carry):
+        @pl.when(k < ny // 2 - 1)
+        def _():
+            take_plane(2, 5, 2 * k + 1, True)
+            take_plane(2, 5, 2 * k + 2, True)
+
+        def one(y, carry):
+            plane(5, 3, y, ("fin", 3), "add")
+            out_copy(3, y).start()
+            return carry
+
+        lax.fori_loop(2 * k, 2 * k + 2, one, 0)
+        to_partner(k).start()
+
+        @pl.when(k > 0)
+        def _():
+            sum_chip(k - 1)
+
+        @pl.when(k > 1)
+        def _():
+            sum_all(k - 2)
+
+        return carry
+
+    pairs = ny // 2
+    lax.fori_loop(0, pairs, last_pair, 0)
+    sum_chip(pairs - 1)
+    sum_all(pairs - 2)
+    sum_all(pairs - 1)
+    for k in range(pairs):
+        back(k, theirs(k)).wait_recv()
+        sens_copy(theirs(k)).start()
+    for k in range(pairs):
+        to_partner(k).wait_send()
+        to_other_chip(k).wait_send()
+        back(k, mine(k)).wait_send()
 
     def settle(y, carry):
         for u in range(3):
@@ -324,6 +460,7 @@
                 copy.wait_send()
         for t in range(4):
             out_copy(t, y).wait()
+        sens_copy(y).wait()
         return carry
 
     lax.fori_loop(0, ny, settle, 0)
@@ -335,21 +472,40 @@
                 for copy in halo(u, side, hs_q.at[u, side], hs_s.at[u, side]):
                     copy.wait_send()
 
-    last.wait()
+    @pl.when(via)
+    def _():
+        for u in range(12):
+            passed_on(u).wait_send()
+
+
+def hand_over(state, total, state_out, total_out, buf, into, onto):
+    phases, ny = state.shape[0], state.shape[2]
+    pieces = [(state.at[t, c], state_out.at[t, c]) for t in range(phases) for c in range(4)] + [(total, total_out)]
+    ins = [pltpu.make_async_copy(a, buf.at[n], into.at[n]) for n, (a, _) in enumerate(pieces)]
+    outs = [pltpu.make_async_copy(buf.at[n], b, onto.at[n]) for n, (_, b) in enumerate(pieces)]
+    for copy in ins:
+        copy.start()
+    for a, b in zip(ins, outs, strict=True):
+        a.wait()
+        b.start()
+    for copy in outs:
+        copy.wait()
 
 
 def on_device(tiles, adjoint_in, velocity, temp_grad, heat_weight, density, cell_kind, inlet):
     phases, _, ny, nx, nz = adjoint_in.shape
     bf16, i16, i32 = jnp.bfloat16, jnp.int16, jnp.int32
     vmem, dma = pltpu.VMEM, pltpu.SemaphoreType.DMA
-    return pl.pallas_call(
+    shapes = (
+        jax.ShapeDtypeStruct(adjoint_in.shape, F32),
+        jax.ShapeDtypeStruct(density.shape, F32),
+    )
+    anywhere = pl.BlockSpec(memory_space=pl.ANY)
+    results = pl.pallas_call(
         functools.partial(kernel, tiles),
-        out_shape=(
-            jax.ShapeDtypeStruct(adjoint_in.shape, F32),
-            jax.ShapeDtypeStruct(density.shape, F32),
-        ),
-        in_specs=[pl.BlockSpec(memory_space=pl.ANY)] * 7,
-        out_specs=[pl.BlockSpec(memory_space=pl.ANY)] * 2,
+        out_shape=shapes,
+        in_specs=[anywhere] * 7,
+        out_specs=[anywhere] * 2,
         scratch_shapes=[
             vmem((6, 4, ny + 2, nx + 2 * PAD, nz), F32),
             vmem((phases, 4, ny, nx, nz), F32),
@@ -364,7 +520,8 @@
             vmem((ny, nx, nz), F32),
             vmem((ny, nx, nz), F32),
             vmem((ny // 2, nx, nz), F32),
-            vmem((2, ny // 2, nx, nz), F32),
+            vmem((ny // 2, nx, nz), F32),
+            vmem((ny // 2, nx, nz), F32),
             vmem((ny, nx, nz), F32),
             vmem((3, ny, 4, nx, nz), i16),
             vmem((3, ny, 8, nz), F32),
@@ -374,19 +531,31 @@
             vmem((12, 2, 8, nz), F32),
             vmem((12, 2, 4, nx, nz), i16),
             vmem((12, 2, 8, nz), F32),
+            vmem((12, nx, nz), i16),
             dma((19,)),
-            dma((phases, ny)),
+            dma((phases + 1, ny)),
             dma((3, ny, 2)),
             dma((3, ny, 2)),
             dma((12, 2, 2)),
             dma((12, 2, 2)),
-            dma((3,)),
-            dma((3,)),
+            dma((3, ny // 2)),
+            dma((3, ny // 2)),
+            dma((12,)),
+            dma((12,)),
         ],
         compiler_params=pltpu.CompilerParams(
             collective_id=0, has_side_effects=True, vmem_limit_bytes=60 * 2**20
         ),
     )(adjoint_in, velocity, temp_grad, heat_weight, density, cell_kind, inlet)
+    pieces = 4 * phases + 1
+    return pl.pallas_call(
+        hand_over,
+        out_shape=shapes,
+        in_specs=[pl.BlockSpec(memory_space=pltpu.HBM)] * 2,
+        out_specs=[anywhere] * 2,
+        scratch_shapes=[vmem((pieces, ny, nx, nz), F32), dma((pieces,)), dma((pieces,))],
+        compiler_params=pltpu.CompilerParams(vmem_limit_bytes=60 * 2**20),
+    )(*results)
 
 
 def solution(mesh):

time: 117 us -> 90 us (0.77)
  Pallas kernels: 107 us -> 89.3 us
  local copies, waits for them, and re-layouts: 8.74 us -> 0 us
    pallas_call x1 -> x2, Pallas kernels: 107 us -> 89.3 us  [the longest x1 82.2 us: on_device(): pl.pallas_call(functools.partial(kernel, tiles), out_shape=shapes, in_spe...]
    unnamed x4 -> x0, local copies, waits for them, and re-layouts: 8.74 us -> none
where the time goes in v2:
time: 90 us; the launch traced here: 89.9 us
  Pallas kernels  89.3 us (99%)
    pallas_call x1, Pallas kernels, on_device(): pl.pallas_call(functools.partial(kernel, tiles), out_shape=shapes, in_spe...  82.2 us
    pallas_call x1, Pallas kernels, on_device(): pl.pallas_call(hand_over, out_shape=shapes, in_specs=[pl.BlockSpec(memory...  7.07 us

profile of v2, /device:TPU:3, one launch (start us, length us, event | category | flops | bytes accessed | tf_op | source)
XLA Modules:
  0.0 89.9 jit_solution(11368664377768433142)
XLA Ops:
  0.6 82.2 %shard_map.86 = (f32[4,4,8,128,128]{4,3,2,1,0:T(8,128)}, f32[8,128,128]{2,1,0:T(8,128)}) custom-call(f32[4,4,8,128,128]{4,3,2,1,0:T(8,128)} %adj.1, bf16[4,3,8,128,128]{4,3,2,1,0:T(8,128)(2,1)} %vel.1, bf16[4,3,8,128,128]{4,3,2,1,0:T(8,128)(2,1)} %grad.1, bf16[4,8,128,128]{3,2,1,0:T(8,128)(2,1)} %heat.1, f32[8,128,128]{2,1,0:T(8,128)} %density.1, ...), custom_call_target="tpu_custom_call" | custom-call | tf_op jit(solution)/shard_map/pallas_call | solution.py:504
  82.8 7.1 %shard_map.87 = (f32[4,4,8,128,128]{4,3,2,1,0:T(8,128)}, f32[8,128,128]{2,1,0:T(8,128)}) custom-call(f32[4,4,8,128,128]{4,3,2,1,0:T(8,128)} %get-tuple-element.4.state, f32[8,128,128]{2,1,0:T(8,128)} %get-tuple-element.5.total), custom_call_target="tpu_custom_call" | custom-call | tf_op jit(solution)/shard_map/pallas_call | solution.py:551

commit v3 on v2

--- a/solution.py
+++ b/solution.py
@@ -1,4 +1,5 @@
 import functools
+import math
 
 import jax
 import jax.numpy as jnp
@@ -11,6 +12,7 @@
 PAD = 8
 BLOCK = 32
 TOP = 32767.0
+TILE = 4096
 MESH = pl.DeviceIdType.MESH
 
 
@@ -21,7 +23,7 @@
 def kernel(
     tiles, adj, vel, grad, heat, density, kind, inlet, out, sens,
     state, fin, v_buf, g_buf, w_buf, d_buf, k_buf, i_buf, cen, nbr, keep, acc, half, near, far, whole,
-    xs_q, xs_s, xr_q, xr_s, hs_q, hs_s, hr_q, hr_s, via_q,
+    xs_q, xs_s, xr_q, xr_s, hs_q, hs_s, hr_q, hr_s, via_q, tiles_of,
     load_sem, out_sem, x_send, x_recv, h_send, h_recv, s_send, s_recv, via_send, via_recv,
 ):
     ny, nx, nz = d_buf.shape
@@ -43,28 +45,38 @@
 
     loads = {}
 
-    def load(name, number, src, dst):
-        loads[name] = pltpu.make_async_copy(src, dst, load_sem.at[number])
-        loads[name].start()
+    def load(name, number, *pairs):
+        for src, dst in pairs:
+            pltpu.make_async_copy(src, dst, load_sem.at[number]).start()
+        loads[name] = (number, tiles_in(*(dst for _, dst in pairs)))
+
+    def tiles_in(*refs):
+        return sum(math.prod(r.shape) * jnp.dtype(r.dtype).itemsize for r in refs) // TILE
+
+    def await_local(sem, n):
+        pltpu.make_async_copy(tiles_of.at[pl.ds(0, n)], tiles_of.at[pl.ds(0, n)], sem).wait()
+
+    def remote_bytes(sem, n):
+        length = tiles_of.at[pl.ds(0, n)]
+        return pltpu.make_async_remote_copy(
+            length, length, sem, sem, device_id=(before, tile), device_id_type=MESH
+        )
+
+    packet = tiles_in(xs_q.at[0, 0], xs_s.at[0, 0])
+
+    def loaded(name):
+        number, size = loads[name]
+        await_local(load_sem.at[number], size)
 
     def load_state(t):
-        load(f"s{t}", t, adj.at[t], state.at[t, :, pl.ds(1, ny), body, :])
+        load(f"state {t}", t, (adj.at[t], state.at[t, :, pl.ds(1, ny), body, :]))
 
     def load_flow(t):
-        load(f"v{t}", 7 + 3 * t, vel.at[t], v_buf.at[t])
-        load(f"g{t}", 8 + 3 * t, grad.at[t], g_buf.at[t])
-        load(f"w{t}", 9 + 3 * t, heat.at[t], w_buf.at[t])
-
+        here = ((vel.at[t], v_buf.at[t]), (grad.at[t], g_buf.at[t]), (heat.at[t], w_buf.at[t]))
+        load(f"flow {t}", 5 + t, *here)
+
+    load_state(2)
     load_state(0)
-    load_state(1)
-    load_state(2)
-    load("density", 4, density, d_buf)
-    load("kind", 5, kind, k_buf)
-    load("inlet", 6, inlet, i_buf)
-    load_flow(0)
-    load_state(3)
-    for t in (1, 2, 3):
-        load_flow(t)
 
     edge = jnp.zeros((PAD, nz), F32)
 
@@ -119,10 +131,10 @@
     def crossing(u, y):
         return [
             pltpu.make_async_remote_copy(
-                a.at[u, y], b.at[u, y], x_send.at[u, y, n], x_recv.at[u, y, n],
+                a.at[u, y], b.at[u, y], x_send.at[0], x_recv.at[u, y],
                 device_id=(before, tile), device_id_type=MESH,
             )
-            for n, (a, b) in enumerate(((xs_q, xr_q), (xs_s, xr_s)))
+            for a, b in ((xs_q, xr_q), (xs_s, xr_s))
         ]
 
     order = iter([(u, (i + ny - 1) % ny) for u in range(3) for i in range(ny)])
@@ -138,10 +150,10 @@
         other = tile + 1 - 2 * side
         return [
             pltpu.make_async_remote_copy(
-                a, b.at[u, side], h_send.at[u, side, n], h_recv.at[u, side, n],
+                a, b.at[side, u], h_send.at[side], h_recv.at[side, u],
                 device_id=(group, other), device_id_type=MESH,
             )
-            for n, (a, b) in enumerate(((q, hr_q), (s, hr_s)))
+            for a, b in ((q, hr_q), (s, hr_s))
         ]
 
     def post(u, side, q, s):
@@ -155,12 +167,12 @@
         @pl.when(far_apart)
         def _():
             pltpu.make_async_remote_copy(
-                q.at[0], hr_q.at[u, side, 0], h_send.at[u, side, 0], h_recv.at[u, side, 0],
+                q.at[0], hr_q.at[side, u, 0], h_send.at[side], h_recv.at[side, u],
                 device_id=(group, tile + 1 - 2 * side), device_id_type=MESH,
             ).start()
             for c, v in enumerate(vias, 1):
                 pltpu.make_async_remote_copy(
-                    q.at[c], via_q.at[u], h_send.at[u, side, 0], via_recv.at[u],
+                    q.at[c], via_q.at[u], h_send.at[side], via_recv.at[u],
                     device_id=(group, (v, tiles - 1 - v)[side]), device_id_type=MESH,
                 ).start()
 
@@ -168,7 +180,7 @@
 
     def passed_on(u):
         return pltpu.make_async_remote_copy(
-            via_q.at[u], hr_q.at[u, 1 - lower, via_part], via_send.at[u], h_recv.at[u, 1 - lower, 0],
+            via_q.at[u], hr_q.at[1 - lower, u, via_part], via_send.at[0], h_recv.at[1 - lower, u],
             device_id=(group, via_to), device_id_type=MESH,
         )
 
@@ -177,7 +189,7 @@
         def _():
             for u in units:
                 pltpu.make_async_remote_copy(
-                    via_q.at[u], via_q.at[u], via_send.at[u], via_recv.at[u],
+                    via_q.at[u], via_q.at[u], via_send.at[0], via_recv.at[u],
                     device_id=(group, via_to), device_id_type=MESH,
                 ).wait_recv()
                 passed_on(u).start()
@@ -187,13 +199,12 @@
 
             @pl.when(there)
             def _():
-                encode(slot, y, hs_q.at[u, side], hs_s.at[u, side])
-                post(u, side, hs_q.at[u, side], hs_s.at[u, side])
+                encode(slot, y, hs_q.at[side, u], hs_s.at[side, u])
+                post(u, side, hs_q.at[side, u], hs_s.at[side, u])
 
     def relay(u, x):
         for side, there, y in ((0, has_up, ny - 1), (1, has_down, 0)):
-            for copy in crossing(x, y):
-                copy.wait_recv()
+            remote_bytes(x_recv.at[x, y], packet).wait_recv()
 
             @pl.when(there)
             def _():
@@ -204,9 +215,8 @@
 
             @pl.when(there)
             def _():
-                for copy in halo(u, side, hs_q.at[u, side], hs_s.at[u, side]):
-                    copy.wait_recv()
-                decode(hr_q.at[u, side], hr_s.at[u, side], slot, row)
+                remote_bytes(h_recv.at[side, u], packet).wait_recv()
+                decode(hr_q.at[side, u], hr_s.at[side, u], slot, row)
 
             @pl.when(jnp.logical_not(there))
             def _():
@@ -215,8 +225,7 @@
 
     def take_plane(x, slot, y, wait):
         if wait:
-            for copy in crossing(x, y):
-                copy.wait_recv()
+            remote_bytes(x_recv.at[x, y], packet).wait_recv()
         decode(xr_q.at[x, y], xr_s.at[x, y], slot, y + 1)
 
     lane = lax.broadcasted_iota(jnp.int32, (BLOCK, nz), 1)
@@ -267,13 +276,27 @@
             state[number, c, y + 1, PAD + x0 : PAD + x0 + BLOCK, :] = value
 
     def out_copy(t, y):
-        return pltpu.make_async_copy(fin.at[t, :, y], out.at[t, :, y], out_sem.at[t, y])
-
-    def chain(slot, t, target, halo_out=None, cross_out=None, total=None, crosses=0):
+        return pltpu.make_async_copy(fin.at[t, :, y], out.at[t, :, y], out_sem.at[t])
+
+    def chain(slot, t, target, halo_in=None, halo_out=None, cross_out=None, total=None, crosses=0, passes=()):
         due = [next(order) for _ in range(crosses)]
 
         def one(i, carry):
-            y = lax.rem(i + ny - 1, ny)
+            for u, at in passes:
+
+                @pl.when(i == at)
+                def _(u=u):
+                    pass_on(u)
+
+            if halo_in is None:
+                y = lax.rem(i + ny - 1, ny)
+            else:
+                y = lax.rem(i + 1, ny)
+
+                @pl.when(i == ny - 2)
+                def _():
+                    take_halo(halo_in, slot)
+
             plane(slot, t, y, target, total)
             if cross_out is not None:
                 encode_crossing(cross_out, target[1], y)
@@ -281,7 +304,7 @@
                 out_copy(t, y).start()
             if halo_out is not None:
 
-                @pl.when(i == 1)
+                @pl.when(i == (1 if halo_in is None else ny - 1))
                 def _():
                     offer(halo_out, target[1])
 
@@ -304,22 +327,30 @@
         take_plane(x, slot, 0, False)
         take_plane(x, slot, ny - 1, False)
 
-    loads["s0"].wait()
+    loaded("state 2")
+    load_state(3)
+    load_state(1)
+    offer(1, 2)
+    loaded("state 0")
+    load("cells", 4, (density, d_buf), (kind, k_buf), (inlet, i_buf))
+    for t in (1, 2, 0, 3):
+        load_flow(t)
 
     def first(i, carry):
         encode_crossing(0, 0, lax.rem(i + ny - 1, ny))
-        return carry
-
-    lax.fori_loop(0, ny, first, 0)
-    for t in (1, 2, 3):
-        loads[f"s{t}"].wait()
-        offer(t - 1, t)
-        if t == 1:
+
+        @pl.when(i == 1)
+        def _():
             cross(*next(order))
             cross(*next(order))
 
-    for name in ("density", "kind", "inlet"):
-        loads[name].wait()
+        return carry
+
+    lax.fori_loop(0, ny, first, 0)
+    for u, t in ((2, 3), (0, 1)):
+        loaded(f"state {t}")
+        offer(u, t)
+    loaded("cells")
 
     def prepare(y, carry):
         rho = rho_of(d_buf[y], k_buf[y])
@@ -334,49 +365,39 @@
     lax.fori_loop(0, ny, prepare, 0)
 
     def ready(t):
-        for n in "vgw":
-            loads[f"{n}{t}"].wait()
+        loaded(f"flow {t}")
 
     S = "state"
-    pass_on(0, 1, 2)
-    ready(0)
-    take_halo(0, 1)
-    chain(1, 0, (S, 4), cross_out=1, crosses=3)
     ready(1)
-    take_halo(1, 2)
-    chain(2, 1, (S, 5), halo_out=3, crosses=3)
-    pass_on(3)
+    chain(2, 1, (S, 5), halo_in=1, halo_out=3, crosses=3, passes=((1, 3), (2, 5), (0, 6)))
     relay(4, 0)
     ready(2)
     take_halo(2, 3)
-    chain(3, 2, (S, 1), halo_out=5, crosses=3)
-    pass_on(4, 5)
-    take_halo(3, 5)
-    chain(5, 0, (S, 4), cross_out=2, crosses=3)
+    chain(3, 2, (S, 2), halo_out=5, crosses=3, passes=((3, 2),))
+    ready(0)
+    take_halo(0, 1)
+    chain(1, 0, (S, 4), cross_out=1, passes=((4, 0), (5, 2)))
     ready(3)
     take_crossing(0, 0)
     take_halo(4, 0)
-    chain(0, 3, (S, 3), halo_out=6, crosses=2)
-    pass_on(6)
-    take_halo(5, 1)
-    chain(1, 1, (S, 2), halo_out=7, crosses=3)
-    pass_on(7)
+    chain(0, 3, (S, 1), halo_out=6, crosses=3)
+    take_halo(3, 5)
+    chain(5, 0, (S, 4), cross_out=2, crosses=3, passes=((6, 2),))
     relay(8, 1)
-    take_halo(6, 3)
-    chain(3, 2, (S, 1), halo_out=9, crosses=3)
-    pass_on(8, 9)
-    take_halo(7, 2)
-    chain(2, 0, ("fin", 0), total="set", crosses=2)
-    take_halo(9, 1)
-    chain(1, 1, ("fin", 1), total="add", crosses=0)
+    take_halo(5, 2)
+    chain(2, 1, (S, 3), halo_out=7, crosses=3, passes=((8, 6),))
+    take_halo(6, 1)
+    chain(1, 2, (S, 5), halo_out=9, crosses=3, passes=((7, 2),))
     take_crossing(1, 0)
     take_halo(8, 0)
-    chain(0, 3, (S, 4), halo_out=10, crosses=0)
-    pass_on(10)
+    chain(0, 3, (S, 4), halo_out=10, crosses=3, passes=((9, 2),))
+    take_halo(7, 3)
+    chain(3, 0, ("fin", 0), total="set", crosses=1, passes=((10, 2),))
     relay(11, 2)
+    take_halo(9, 5)
+    chain(5, 1, ("fin", 1), total="add", passes=((11, 6),))
     take_halo(10, 4)
-    chain(4, 2, ("fin", 2), total="add", crosses=0)
-    pass_on(11)
+    chain(4, 2, ("fin", 2), total="add")
 
     def mine(k):
         return 2 * k + core
@@ -386,7 +407,7 @@
 
     def send(n, k, src, dst, other):
         return pltpu.make_async_remote_copy(
-            src, dst, s_send.at[n, k], s_recv.at[n, k], device_id=(other, tile), device_id_type=MESH
+            src, dst, s_send.at[0], s_recv.at[n, k], device_id=(other, tile), device_id_type=MESH
         )
 
     def to_partner(k):
@@ -399,7 +420,7 @@
         return send(2, k, whole.at[y], whole.at[y], partner)
 
     def sens_copy(y):
-        return pltpu.make_async_copy(whole.at[y], sens.at[y], out_sem.at[4, y])
+        return pltpu.make_async_copy(whole.at[y], sens.at[y], out_sem.at[4])
 
     def sum_chip(k):
         to_partner(k).wait_recv()
@@ -413,18 +434,18 @@
         back(k, y).start()
         sens_copy(y).start()
 
-    take_halo(11, 5)
-    take_plane(2, 5, 0, False)
-    take_plane(2, 5, ny - 1, False)
+    take_halo(11, 0)
+    take_plane(2, 0, 0, False)
+    take_plane(2, 0, ny - 1, False)
 
     def last_pair(k, carry):
         @pl.when(k < ny // 2 - 1)
         def _():
-            take_plane(2, 5, 2 * k + 1, True)
-            take_plane(2, 5, 2 * k + 2, True)
+            take_plane(2, 0, 2 * k + 1, True)
+            take_plane(2, 0, 2 * k + 2, True)
 
         def one(y, carry):
-            plane(5, 3, y, ("fin", 3), "add")
+            plane(0, 3, y, ("fin", 3), "add")
             out_copy(3, y).start()
             return carry
 
@@ -449,33 +470,25 @@
     for k in range(pairs):
         back(k, theirs(k)).wait_recv()
         sens_copy(theirs(k)).start()
-    for k in range(pairs):
-        to_partner(k).wait_send()
-        to_other_chip(k).wait_send()
-        back(k, mine(k)).wait_send()
-
-    def settle(y, carry):
-        for u in range(3):
-            for copy in crossing(u, y):
-                copy.wait_send()
-        for t in range(4):
-            out_copy(t, y).wait()
-        sens_copy(y).wait()
-        return carry
-
-    lax.fori_loop(0, ny, settle, 0)
+
+    def sent(sem, *refs):
+        remote_bytes(sem, tiles_in(*refs)).wait_send()
+
+    sent(s_send.at[0], near, far, half)
+    sent(x_send.at[0], xs_q, xs_s)
     for side, there in ((0, has_up), (1, has_down)):
 
         @pl.when(there)
         def _():
-            for u in range(12):
-                for copy in halo(u, side, hs_q.at[u, side], hs_s.at[u, side]):
-                    copy.wait_send()
+            sent(h_send.at[side], hs_q.at[side], hs_s.at[side])
 
     @pl.when(via)
     def _():
-        for u in range(12):
-            passed_on(u).wait_send()
+        sent(via_send.at[0], via_q)
+
+    for t in range(4):
+        pltpu.make_async_copy(fin.at[t], out.at[t], out_sem.at[t]).wait()
+    pltpu.make_async_copy(whole, sens, out_sem.at[4]).wait()
 
 
 def hand_over(state, total, state_out, total_out, buf, into, onto):
@@ -527,20 +540,21 @@
             vmem((3, ny, 8, nz), F32),
             vmem((3, ny, 4, nx, nz), i16),
             vmem((3, ny, 8, nz), F32),
-            vmem((12, 2, 4, nx, nz), i16),
-            vmem((12, 2, 8, nz), F32),
-            vmem((12, 2, 4, nx, nz), i16),
-            vmem((12, 2, 8, nz), F32),
+            vmem((2, 12, 4, nx, nz), i16),
+            vmem((2, 12, 8, nz), F32),
+            vmem((2, 12, 4, nx, nz), i16),
+            vmem((2, 12, 8, nz), F32),
             vmem((12, nx, nz), i16),
-            dma((19,)),
-            dma((phases + 1, ny)),
-            dma((3, ny, 2)),
-            dma((3, ny, 2)),
-            dma((12, 2, 2)),
-            dma((12, 2, 2)),
+            vmem((24 * (8 * nx * nz // TILE + 1), TILE // (4 * nz), nz), F32),
+            dma((9,)),
+            dma((5,)),
+            dma((1,)),
+            dma((3, ny)),
+            dma((2,)),
+            dma((2, 12)),
+            dma((1,)),
             dma((3, ny // 2)),
-            dma((3, ny // 2)),
-            dma((12,)),
+            dma((1,)),
             dma((12,)),
         ],
         compiler_params=pltpu.CompilerParams(

time: 90 us -> 84.6 us (0.940)
  Pallas kernels: 89.3 us -> 83.6 us
    pallas_call x1, Pallas kernels: 82.2 us -> 76.5 us  [on_device(): pl.pallas_call(functools.partial(kernel, tiles), out_shape=shapes, in_spe...]
where the time goes in v3:
time: 84.6 us; the launch traced here: 84.2 us
  Pallas kernels  83.6 us (99%)
    pallas_call x1, Pallas kernels, on_device(): pl.pallas_call(functools.partial(kernel, tiles), out_shape=shapes, in_spe...  76.5 us
    pallas_call x1, Pallas kernels, on_device(): pl.pallas_call(hand_over, out_shape=shapes, in_specs=[pl.BlockSpec(memory...  7.07 us

profile of v3, /device:TPU:3, one launch (start us, length us, event | category | flops | bytes accessed | tf_op | source)
XLA Modules:
  0.0 84.2 jit_solution(10701164769899829582)
XLA Ops:
  0.6 76.5 %shard_map.86 = (f32[4,4,8,128,128]{4,3,2,1,0:T(8,128)}, f32[8,128,128]{2,1,0:T(8,128)}) custom-call(f32[4,4,8,128,128]{4,3,2,1,0:T(8,128)} %adj.1, bf16[4,3,8,128,128]{4,3,2,1,0:T(8,128)(2,1)} %vel.1, bf16[4,3,8,128,128]{4,3,2,1,0:T(8,128)(2,1)} %grad.1, bf16[4,8,128,128]{3,2,1,0:T(8,128)(2,1)} %heat.1, f32[8,128,128]{2,1,0:T(8,128)} %density.1, ...), custom_call_target="tpu_custom_call" | custom-call | tf_op jit(solution)/shard_map/pallas_call | solution.py:517
  77.1 7.1 %shard_map.87 = (f32[4,4,8,128,128]{4,3,2,1,0:T(8,128)}, f32[8,128,128]{2,1,0:T(8,128)}) custom-call(f32[4,4,8,128,128]{4,3,2,1,0:T(8,128)} %get-tuple-element.4.state, f32[8,128,128]{2,1,0:T(8,128)} %get-tuple-element.5.total), custom_call_target="tpu_custom_call" | custom-call | tf_op jit(solution)/shard_map/pallas_call | solution.py:565

commit v4 on v3

--- a/solution.py
+++ b/solution.py
@@ -310,7 +310,7 @@
 
             for n, (u, plane_of) in enumerate(due):
 
-                @pl.when(i == 2 + 2 * n)
+                @pl.when(i == (3, 6)[n])
                 def _(u=u, plane_of=plane_of):
                     cross(u, plane_of)
 
@@ -369,35 +369,35 @@
 
     S = "state"
     ready(1)
-    chain(2, 1, (S, 5), halo_in=1, halo_out=3, crosses=3, passes=((1, 3), (2, 5), (0, 6)))
+    chain(2, 1, (S, 5), halo_in=1, halo_out=3, passes=((1, 3), (2, 5), (0, 6)), crosses=2)
     relay(4, 0)
     ready(2)
     take_halo(2, 3)
-    chain(3, 2, (S, 2), halo_out=5, crosses=3, passes=((3, 2),))
+    chain(3, 2, (S, 2), halo_out=5, passes=((3, 5),), crosses=2)
     ready(0)
     take_halo(0, 1)
-    chain(1, 0, (S, 4), cross_out=1, passes=((4, 0), (5, 2)))
+    chain(1, 0, (S, 4), cross_out=1, passes=((4, 0), (5, 5)), crosses=2)
     ready(3)
     take_crossing(0, 0)
     take_halo(4, 0)
-    chain(0, 3, (S, 1), halo_out=6, crosses=3)
+    chain(0, 3, (S, 1), halo_out=6, crosses=2)
     take_halo(3, 5)
-    chain(5, 0, (S, 4), cross_out=2, crosses=3, passes=((6, 2),))
+    chain(5, 0, (S, 4), cross_out=2, passes=((6, 5),), crosses=2)
     relay(8, 1)
     take_halo(5, 2)
-    chain(2, 1, (S, 3), halo_out=7, crosses=3, passes=((8, 6),))
+    chain(2, 1, (S, 3), halo_out=7, passes=((8, 6),), crosses=2)
     take_halo(6, 1)
-    chain(1, 2, (S, 5), halo_out=9, crosses=3, passes=((7, 2),))
+    chain(1, 2, (S, 5), halo_out=9, passes=((7, 5),), crosses=2)
     take_crossing(1, 0)
     take_halo(8, 0)
-    chain(0, 3, (S, 4), halo_out=10, crosses=3, passes=((9, 2),))
+    chain(0, 3, (S, 4), halo_out=10, passes=((9, 5),), crosses=2)
     take_halo(7, 3)
-    chain(3, 0, ("fin", 0), total="set", crosses=1, passes=((10, 2),))
+    chain(3, 0, ("fin", 0), total="set", passes=((10, 5),), crosses=2)
     relay(11, 2)
     take_halo(9, 5)
-    chain(5, 1, ("fin", 1), total="add", passes=((11, 6),))
+    chain(5, 1, ("fin", 1), total="add", passes=((11, 6),), crosses=2)
     take_halo(10, 4)
-    chain(4, 2, ("fin", 2), total="add")
+    chain(4, 2, ("fin", 2), total="add", crosses=2)
 
     def mine(k):
         return 2 * k + core

time: 84.6 us -> 78.7 us (0.930)
  Pallas kernels: 83.6 us -> 76.9 us
    pallas_call x1, Pallas kernels: 76.5 us -> 69.9 us  [on_device(): pl.pallas_call(functools.partial(kernel, tiles), out_shape=shapes, in_spe...]
where the time goes in v4:
time: 78.7 us; the launch traced here: 77.6 us
  Pallas kernels  76.9 us (98%)
    pallas_call x1, Pallas kernels, on_device(): pl.pallas_call(functools.partial(kernel, tiles), out_shape=shapes, in_spe...  69.9 us
    pallas_call x1, Pallas kernels, on_device(): pl.pallas_call(hand_over, out_shape=shapes, in_specs=[pl.BlockSpec(memory...  7.07 us

profile of v4, /device:TPU:3, one launch (start us, length us, event | category | flops | bytes accessed | tf_op | source)
XLA Modules:
  0.0 77.6 jit_solution(9710439567205645059)
XLA Ops:
  0.6 69.9 %shard_map.86 = (f32[4,4,8,128,128]{4,3,2,1,0:T(8,128)}, f32[8,128,128]{2,1,0:T(8,128)}) custom-call(f32[4,4,8,128,128]{4,3,2,1,0:T(8,128)} %adj.1, bf16[4,3,8,128,128]{4,3,2,1,0:T(8,128)(2,1)} %vel.1, bf16[4,3,8,128,128]{4,3,2,1,0:T(8,128)(2,1)} %grad.1, bf16[4,8,128,128]{3,2,1,0:T(8,128)(2,1)} %heat.1, f32[8,128,128]{2,1,0:T(8,128)} %density.1, ...), custom_call_target="tpu_custom_call" | custom-call | tf_op jit(solution)/shard_map/pallas_call | solution.py:517
  70.5 7.1 %shard_map.87 = (f32[4,4,8,128,128]{4,3,2,1,0:T(8,128)}, f32[8,128,128]{2,1,0:T(8,128)}) custom-call(f32[4,4,8,128,128]{4,3,2,1,0:T(8,128)} %get-tuple-element.4.state, f32[8,128,128]{2,1,0:T(8,128)} %get-tuple-element.5.total), custom_call_target="tpu_custom_call" | custom-call | tf_op jit(solution)/shard_map/pallas_call | solution.py:565

commit v5 on v4

--- a/solution.py
+++ b/solution.py
@@ -271,12 +271,12 @@
     def put(target, c, y, x0, value):
         kind_of, number = target
         if kind_of == "fin":
-            fin[number, c, y, x0 : x0 + BLOCK, :] = value
+            fin[number % 2, c, y, x0 : x0 + BLOCK, :] = value
         else:
             state[number, c, y + 1, PAD + x0 : PAD + x0 + BLOCK, :] = value
 
     def out_copy(t, y):
-        return pltpu.make_async_copy(fin.at[t, :, y], out.at[t, :, y], out_sem.at[t])
+        return pltpu.make_async_copy(fin.at[t % 2, :, y], out.at[t, :, y], out_sem.at[t])
 
     def chain(slot, t, target, halo_in=None, halo_out=None, cross_out=None, total=None, crosses=0, passes=()):
         due = [next(order) for _ in range(crosses)]
@@ -317,6 +317,9 @@
             return carry
 
         lax.fori_loop(0, ny, one, 0)
+
+    def written(t):
+        pltpu.make_async_copy(fin.at[t % 2], out.at[t], out_sem.at[t]).wait()
 
     def take_crossing(x, slot):
         def one(i, carry):
@@ -396,6 +399,7 @@
     relay(11, 2)
     take_halo(9, 5)
     chain(5, 1, ("fin", 1), total="add", passes=((11, 6),), crosses=2)
+    written(0)
     take_halo(10, 4)
     chain(4, 2, ("fin", 2), total="add", crosses=2)
 
@@ -434,6 +438,7 @@
         back(k, y).start()
         sens_copy(y).start()
 
+    written(1)
     take_halo(11, 0)
     take_plane(2, 0, 0, False)
     take_plane(2, 0, ny - 1, False)
@@ -486,22 +491,18 @@
     def _():
         sent(via_send.at[0], via_q)
 
-    for t in range(4):
-        pltpu.make_async_copy(fin.at[t], out.at[t], out_sem.at[t]).wait()
+    written(2)
+    written(3)
     pltpu.make_async_copy(whole, sens, out_sem.at[4]).wait()
 
 
-def hand_over(state, total, state_out, total_out, buf, into, onto):
-    phases, ny = state.shape[0], state.shape[2]
-    pieces = [(state.at[t, c], state_out.at[t, c]) for t in range(phases) for c in range(4)] + [(total, total_out)]
-    ins = [pltpu.make_async_copy(a, buf.at[n], into.at[n]) for n, (a, _) in enumerate(pieces)]
-    outs = [pltpu.make_async_copy(buf.at[n], b, onto.at[n]) for n, (_, b) in enumerate(pieces)]
-    for copy in ins:
+def hand_over(state, total, state_out, total_out, sems):
+    phases = state.shape[0]
+    copies = [pltpu.make_async_copy(state.at[t], state_out.at[t], sems.at[t]) for t in range(phases)]
+    copies.append(pltpu.make_async_copy(total, total_out, sems.at[phases]))
+    for copy in copies:
         copy.start()
-    for a, b in zip(ins, outs, strict=True):
-        a.wait()
-        b.start()
-    for copy in outs:
+    for copy in copies:
         copy.wait()
 
 
@@ -521,7 +522,7 @@
         out_specs=[anywhere] * 2,
         scratch_shapes=[
             vmem((6, 4, ny + 2, nx + 2 * PAD, nz), F32),
-            vmem((phases, 4, ny, nx, nz), F32),
+            vmem((2, 4, ny, nx, nz), F32),
             vmem((phases, 3, ny, nx, nz), bf16),
             vmem((phases, 3, ny, nx, nz), bf16),
             vmem((phases, ny, nx, nz), bf16),
@@ -558,17 +559,16 @@
             dma((12,)),
         ],
         compiler_params=pltpu.CompilerParams(
-            collective_id=0, has_side_effects=True, vmem_limit_bytes=60 * 2**20
+            collective_id=0, has_side_effects=True, vmem_limit_bytes=53 * 2**20
         ),
     )(adjoint_in, velocity, temp_grad, heat_weight, density, cell_kind, inlet)
-    pieces = 4 * phases + 1
     return pl.pallas_call(
         hand_over,
         out_shape=shapes,
-        in_specs=[pl.BlockSpec(memory_space=pltpu.HBM)] * 2,
+        in_specs=[anywhere] * 2,
         out_specs=[anywhere] * 2,
-        scratch_shapes=[vmem((pieces, ny, nx, nz), F32), dma((pieces,)), dma((pieces,))],
-        compiler_params=pltpu.CompilerParams(vmem_limit_bytes=60 * 2**20),
+        scratch_shapes=[dma((phases + 1,))],
+        compiler_params=pltpu.CompilerParams(vmem_limit_bytes=4 * 2**20),
     )(*results)
 
 

time: 78.7 us -> 78.1 us (level)
  Pallas kernels: 76.9 us -> 72.8 us
  local copies, waits for them, and re-layouts: 0 us -> 3.37 us
    pallas_call x1, Pallas kernels: 7.07 us -> 3.48 us  [on_device(): pl.pallas_call(hand_over, out_shape=shapes, in_specs=[anywhere] * 2, out_...]
    unnamed x0 -> x2, local copies, waits for them, and re-layouts: none -> 3.37 us
where the time goes in v5:
time: 78.1 us; the launch traced here: 76.9 us
  Pallas kernels  72.8 us (93%)
  local copies, waits for them, and re-layouts  3.37 us (4%)
    pallas_call x1, Pallas kernels, on_device(): pl.pallas_call(functools.partial(kernel, tiles), out_shape=shapes, in_spe...  69.4 us
    pallas_call x1, Pallas kernels, on_device(): pl.pallas_call(hand_over, out_shape=shapes, in_specs=[anywhere] * 2, out_...  3.48 us
    unnamed x2, local copies, waits for them, and re-layouts  3.37 us

profile of v5, /device:TPU:3, one launch (start us, length us, event | category | flops | bytes accessed | tf_op | source)
XLA Modules:
  0.0 76.9 jit_solution(18222793577812021957)
XLA Ops:
  0.6 69.4 %shard_map.86 = (f32[4,4,8,128,128]{4,3,2,1,0:T(8,128)}, f32[8,128,128]{2,1,0:T(8,128)S(1)}) custom-call(f32[4,4,8,128,128]{4,3,2,1,0:T(8,128)} %adj.1, bf16[4,3,8,128,128]{4,3,2,1,0:T(8,128)(2,1)} %vel.1, bf16[4,3,8,128,128]{4,3,2,1,0:T(8,128)(2,1)} %grad.1, bf16[4,8,128,128]{3,2,1,0:T(8,128)(2,1)} %heat.1, f32[8,128,128]{2,1,0:T(8,128)} %density.1, ...), custom_call_target="tpu_custom_call" | custom-call | tf_op jit(solution)/shard_map/pallas_call | solution.py:518
  70.0 0.0 copy-start
  70.0 3.4 %copy-done = f32[4,4,8,128,128]{4,3,2,1,0:T(8,128)S(1)} copy-done((f32[4,4,8,128,128]{4,3,2,1,0:T(8,128)S(1)}, f32[4,4,8,128,128]{4,3,2,1,0:T(8,128)}, u32[]{:S(2)}) %copy-start) | copy-done | bytes 8388632
  73.4 3.5 %shard_map.87 = (f32[4,4,8,128,128]{4,3,2,1,0:T(8,128)}, f32[8,128,128]{2,1,0:T(8,128)}) custom-call(f32[4,4,8,128,128]{4,3,2,1,0:T(8,128)S(1)} %copy-done, f32[8,128,128]{2,1,0:T(8,128)S(1)} %get-tuple-element.5.total), custom_call_target="tpu_custom_call" | custom-call | tf_op jit(solution)/shard_map/pallas_call | solution.py:565
Async XLA Ops:
  70.0 3.4 %copy-start = (f32[4,4,8,128,128]{4,3,2,1,0:T(8,128)S(1)}, f32[4,4,8,128,128]{4,3,2,1,0:T(8,128)}, u32[]{:S(2)}) copy-start(f32[4,4,8,128,128]{4,3,2,1,0:T(8,128)} %get-tuple-element.4.state) | copy-start | bytes 25165828

commit v6 on v5

--- a/solution.py
+++ b/solution.py
@@ -166,15 +166,15 @@
 
         @pl.when(far_apart)
         def _():
-            pltpu.make_async_remote_copy(
-                q.at[0], hr_q.at[side, u, 0], h_send.at[side], h_recv.at[side, u],
-                device_id=(group, tile + 1 - 2 * side), device_id_type=MESH,
-            ).start()
             for c, v in enumerate(vias, 1):
                 pltpu.make_async_remote_copy(
                     q.at[c], via_q.at[u], h_send.at[side], via_recv.at[u],
                     device_id=(group, (v, tiles - 1 - v)[side]), device_id_type=MESH,
                 ).start()
+            pltpu.make_async_remote_copy(
+                q.at[0], hr_q.at[side, u, 0], h_send.at[side], h_recv.at[side, u],
+                device_id=(group, tile + 1 - 2 * side), device_id_type=MESH,
+            ).start()
 
         scale.start()
 

time: 78.1 us -> 78.1 us (level)
  no operation moved by 1% of the time
where the time goes in v6:
time: 78.1 us; the launch traced here: 76.9 us
  Pallas kernels  72.8 us (93%)
  local copies, waits for them, and re-layouts  3.37 us (4%)
    pallas_call x1, Pallas kernels, on_device(): pl.pallas_call(functools.partial(kernel, tiles), out_shape=shapes, in_spe...  69.4 us
    pallas_call x1, Pallas kernels, on_device(): pl.pallas_call(hand_over, out_shape=shapes, in_specs=[anywhere] * 2, out_...  3.48 us
    unnamed x2, local copies, waits for them, and re-layouts  3.37 us

profile of v6, /device:TPU:3, one launch (start us, length us, event | category | flops | bytes accessed | tf_op | source)
XLA Modules:
  0.0 76.9 jit_solution(11131792269268940025)
XLA Ops:
  0.6 69.4 %shard_map.86 = (f32[4,4,8,128,128]{4,3,2,1,0:T(8,128)}, f32[8,128,128]{2,1,0:T(8,128)S(1)}) custom-call(f32[4,4,8,128,128]{4,3,2,1,0:T(8,128)} %adj.1, bf16[4,3,8,128,128]{4,3,2,1,0:T(8,128)(2,1)} %vel.1, bf16[4,3,8,128,128]{4,3,2,1,0:T(8,128)(2,1)} %grad.1, bf16[4,8,128,128]{3,2,1,0:T(8,128)(2,1)} %heat.1, f32[8,128,128]{2,1,0:T(8,128)} %density.1, ...), custom_call_target="tpu_custom_call" | custom-call | tf_op jit(solution)/shard_map/pallas_call | solution.py:518
  70.0 0.0 copy-start
  70.0 3.4 %copy-done = f32[4,4,8,128,128]{4,3,2,1,0:T(8,128)S(1)} copy-done((f32[4,4,8,128,128]{4,3,2,1,0:T(8,128)S(1)}, f32[4,4,8,128,128]{4,3,2,1,0:T(8,128)}, u32[]{:S(2)}) %copy-start) | copy-done | bytes 8388632
  73.4 3.5 %shard_map.87 = (f32[4,4,8,128,128]{4,3,2,1,0:T(8,128)}, f32[8,128,128]{2,1,0:T(8,128)}) custom-call(f32[4,4,8,128,128]{4,3,2,1,0:T(8,128)S(1)} %copy-done, f32[8,128,128]{2,1,0:T(8,128)S(1)} %get-tuple-element.5.total), custom_call_target="tpu_custom_call" | custom-call | tf_op jit(solution)/shard_map/pallas_call | solution.py:565
Async XLA Ops:
  70.0 3.4 %copy-start = (f32[4,4,8,128,128]{4,3,2,1,0:T(8,128)S(1)}, f32[4,4,8,128,128]{4,3,2,1,0:T(8,128)}, u32[]{:S(2)}) copy-start(f32[4,4,8,128,128]{4,3,2,1,0:T(8,128)} %get-tuple-element.4.state) | copy-start | bytes 25165828
